TPU v7x, 32 devices: a whole 2x2x4 slice. The times are simulated.
32 devices in a mesh: dp: 2 (over core), ctx: 16 (over z, y, x).
Axes of the slice: x: 2, y: 2, z: 4, core: 2. Of those that a mesh axis runs over, the one named last changes fastest.
Arguments:
- queries: bfloat16 [8192, 1536], P(('dp', 'ctx')), parts along dimension 0, may hold values from -53 to 53
- keys: bfloat16 [8192, 1536], P(('dp', 'ctx')), parts along dimension 0, may hold values from -6 to 6
- values: bfloat16 [8192, 1536], P(('dp', 'ctx')), parts along dimension 0, may hold values from -6 to 6
- grad_out: bfloat16 [8192, 1536], P(('dp', 'ctx')), parts along dimension 0, may hold values from -6 to 6
- summary_lists: int32 [64, 4], P('dp'), parts along dimension 0, may hold values from 0 to 7, as said below
Outputs:
- attended: bfloat16 [8192, 1536], P(('dp', 'ctx')), parts along dimension 0
- grad_queries: bfloat16 [8192, 1536], P(('dp', 'ctx')), parts along dimension 0
- grad_keys: bfloat16 [8192, 1536], P(('dp', 'ctx')), parts along dimension 0
- grad_values: bfloat16 [8192, 1536], P(('dp', 'ctx')), parts along dimension 0
There are 2 independent parts, one for each index of `dp`. A program takes and returns all parts, laid end to end along the dimension named above; each array names one. Nothing has to cross between parts.
Inputs may be any that keep to these rules, and one draw needn't show every extreme that they name: `summary_lists`: each row names 4 different summary numbers.
All inputs are finite; a program needn't handle non-finite values.
Results may differ from a plain program's by a relative error of at most 0.019.
Values may be sent and summed in bfloat16 or wider, within the bound.
A program may use at most 192 MiB of HBM per device.

v0:
```python
import jax
import jax.numpy as jnp
import numpy as np
from jax import lax
from jax.sharding import PartitionSpec as P

H = 12
HS = 128
BLK = 128
SUMS = 8
PICKS = 4


def extended_2(shard, sides, width):
    for axis, dim in sides:
        size, length = (lax.axis_size(axis), shard.shape[dim])
        up = [(i, (i + 1) % size) for i in range(size - 1)]
        down = [(j, i) for i, j in up]
        last = lax.slice_in_dim(shard, length - width, length, axis=dim)
        initial = lax.slice_in_dim(shard, 0, width, axis=dim)
        before = lax.ppermute(last, axis, up)
        after = lax.ppermute(initial, axis, down)
        shard = jnp.concatenate([before, shard, after], axis=dim)
    return shard


def from_root(value, axis, source):
    kept = jnp.where(lax.axis_index(axis) == source, value, 0).astype(value.dtype)
    return lax.psum(kept, axis)


def attend(query_blk, key_rows, value_rows, grad_blk, visible, scale):
    scores = (
        jnp.einsum("gqhd,gkhd->ghqk", query_blk, key_rows, preferred_element_type=jnp.float32)
        * scale
    )
    scores = jnp.where(visible[:, None], scores, -1e30)
    highest = jnp.max(scores, axis=-1, keepdims=True)
    weights = jnp.where(visible[:, None], jnp.exp(scores - highest), 0.0)
    probs = weights / jnp.sum(weights, axis=-1, keepdims=True)
    probs_low = probs.astype(jnp.bfloat16)
    attended = jnp.einsum(
        "ghqk,gkhd->gqhd", probs_low, value_rows, preferred_element_type=jnp.float32
    ).astype(jnp.bfloat16)
    delta = jnp.sum(grad_blk.astype(jnp.float32) * attended.astype(jnp.float32), axis=-1)
    dprob = jnp.einsum("gqhd,gkhd->ghqk", grad_blk, value_rows, preferred_element_type=jnp.float32)
    dscore = (probs * (dprob - jnp.transpose(delta, (0, 2, 1))[..., None])).astype(jnp.bfloat16)
    grad_query = (
        jnp.einsum("ghqk,gkhd->gqhd", dscore, key_rows, preferred_element_type=jnp.float32) * scale
    ).astype(jnp.bfloat16)
    grad_key = (
        jnp.einsum("ghqk,gqhd->gkhd", dscore, query_blk, preferred_element_type=jnp.float32) * scale
    )
    grad_value = jnp.einsum(
        "ghqk,gqhd->gkhd", probs_low, grad_blk, preferred_element_type=jnp.float32
    )
    return (attended, grad_query, grad_key, grad_value)


def on_device(queries, keys, values, grad_out, summary_lists):
    tok_rows, feat_width = queries.shape
    ctx_count = lax.axis_size("ctx")
    ctx_here = lax.axis_index("ctx")
    slot_count = tok_rows // BLK
    half_slots = slot_count // 2
    stride = slot_count * ctx_count // SUMS
    kcount = 2 + PICKS
    scale = HS ** (-0.5)
    key_blocks = keys.reshape(slot_count, BLK, feat_width)
    value_blocks = values.reshape(slot_count, BLK, feat_width)
    query_blocks = queries.reshape(slot_count, BLK, H, HS)
    grad_blocks = grad_out.reshape(slot_count, BLK, H, HS)
    slot_ids = jnp.arange(slot_count, dtype=jnp.int32)
    doc_block = jnp.where(
        slot_ids < half_slots,
        ctx_here * half_slots + slot_ids,
        (2 * ctx_count - 1 - ctx_here) * half_slots + slot_ids - half_slots,
    )
    on_last = ctx_here == ctx_count - 1
    edges = jnp.stack(
        [
            jnp.stack([key_blocks[slot_count - 1], value_blocks[slot_count - 1]]),
            jnp.stack([key_blocks[half_slots - 1], value_blocks[half_slots - 1]]),
        ]
    )
    extended = extended_2(edges, (("ctx", 0),), 1)
    upper_prev = jnp.where(on_last, edges[1], extended[3])
    prev_keys = jnp.concatenate(
        [
            extended[0, 0][None],
            key_blocks[: half_slots - 1],
            upper_prev[0][None],
            key_blocks[half_slots : slot_count - 1],
        ]
    )
    prev_values = jnp.concatenate(
        [
            extended[0, 1][None],
            value_blocks[: half_slots - 1],
            upper_prev[1][None],
            value_blocks[half_slots : slot_count - 1],
        ]
    )
    prev_live = doc_block >= 1
    owner_list = []
    slot_list = []
    for summary in range(SUMS):
        summary_block = summary * stride + stride - 1
        span_id = summary_block // half_slots
        if span_id < ctx_count:
            owner_list.append(span_id)
            slot_list.append(summary_block - span_id * half_slots)
        else:
            owner_list.append(2 * ctx_count - 1 - span_id)
            slot_list.append(summary_block - span_id * half_slots + half_slots)
    owner_slots = np.array(slot_list, dtype=np.int32)
    owner_array = np.array(owner_list, dtype=np.int32)
    is_owner = (ctx_here == jnp.asarray(owner_array)).astype(jnp.float32)[:, None, None]
    shared_keys = []
    shared_values = []
    for summary in range(SUMS):
        got_key, got_value = (
            from_root(key_blocks[slot_list[summary]], "ctx", owner_list[summary]),
            from_root(value_blocks[slot_list[summary]], "ctx", owner_list[summary]),
        )
        shared_keys.append(got_key)
        shared_values.append(got_value)
    summary_keys = jnp.stack(shared_keys)
    summary_values = jnp.stack(shared_values)
    picks = summary_lists[doc_block]
    pick_live = picks * stride + stride - 1 < doc_block[:, None] - 1
    chosen_keys = summary_keys[picks]
    chosen_values = summary_values[picks]
    pick_onehot = (
        (picks[..., None] == jnp.arange(SUMS, dtype=jnp.int32)) & pick_live[..., None]
    ).astype(jnp.float32)
    causal = jnp.arange(BLK)[:, None] >= jnp.arange(BLK)[None, :]
    live_all = jnp.concatenate(
        [prev_live[:, None], jnp.ones((slot_count, 1), bool), pick_live], axis=1
    )
    kinds = jnp.arange(kcount)[None, :, None, None]
    visible_all = jnp.where(kinds == 1, causal[None, None], live_all[:, :, None, None])
    visible_all = jnp.transpose(visible_all, (0, 2, 1, 3)).reshape(slot_count, BLK, kcount * BLK)
    group_size = min(4, slot_count)
    out_parts, dq_parts = ([], [])
    own_gk, own_gv, prev_gk, prev_gv = ([], [], [], [])
    group_keys = jnp.concatenate(
        [prev_keys[0:group_size, None], key_blocks[0:group_size, None], chosen_keys], axis=1
    ).reshape(group_size, kcount * BLK, H, HS)
    group_values = jnp.concatenate(
        [prev_values[0:group_size, None], value_blocks[0:group_size, None], chosen_values], axis=1
    ).reshape(group_size, kcount * BLK, H, HS)
    attended, grad_query, grad_key, grad_value = attend(
        query_blocks, group_keys, group_values, grad_blocks, visible_all, scale
    )
    grad_key = grad_key.reshape(group_size, kcount, BLK, feat_width)
    grad_value = grad_value.reshape(group_size, kcount, BLK, feat_width)
    out_parts.append(attended)
    dq_parts.append(grad_query)
    own_gk.append(grad_key[:, 1])
    own_gv.append(grad_value[:, 1])
    prev_gk.append(grad_key[:, 0])
    prev_gv.append(grad_value[:, 0])
    summary_gk = jnp.einsum(
        "gps,gpbc->sbc", pick_onehot, grad_key[:, 2:], precision=lax.Precision.HIGHEST
    )
    summary_gv = jnp.einsum(
        "gps,gpbc->sbc", pick_onehot, grad_value[:, 2:], precision=lax.Precision.HIGHEST
    )
    acc_keys = own_gk[0]
    acc_values = own_gv[0]
    prev_k = prev_gk[0]
    prev_v = prev_gv[0]
    zero_block = jnp.zeros((1, BLK, feat_width), jnp.float32)
    acc_keys = acc_keys + jnp.concatenate(
        [prev_k[1:half_slots], zero_block, prev_k[half_slots + 1 :], zero_block]
    )
    acc_values = acc_values + jnp.concatenate(
        [prev_v[1:half_slots], zero_block, prev_v[half_slots + 1 :], zero_block]
    )
    upper_grad = jnp.stack([prev_k[half_slots], prev_v[half_slots]])
    front_grad = jnp.stack([prev_k[0], prev_v[0]])
    local_back = jnp.where(on_last, upper_grad, 0.0)
    sent_back = jnp.where(on_last, 0.0, upper_grad)
    returned = extended_2(jnp.stack([front_grad, sent_back]), (("ctx", 0),), 1)
    acc_keys = acc_keys.at[half_slots - 1].add(local_back[0] + returned[3, 0])
    acc_values = acc_values.at[half_slots - 1].add(local_back[1] + returned[3, 1])
    acc_keys = acc_keys.at[slot_count - 1].add(returned[0, 0])
    acc_values = acc_values.at[slot_count - 1].add(returned[0, 1])
    total_keys, total_values = lax.psum((summary_gk, summary_gv), "ctx")
    acc_keys = acc_keys.at[owner_slots].add(total_keys * is_owner)
    acc_values = acc_values.at[owner_slots].add(total_values * is_owner)
    attended_all = out_parts[0].reshape(tok_rows, feat_width)
    grad_q_all = dq_parts[0].reshape(tok_rows, feat_width)
    return (
        attended_all,
        grad_q_all,
        acc_keys.astype(jnp.bfloat16).reshape(tok_rows, feat_width),
        acc_values.astype(jnp.bfloat16).reshape(tok_rows, feat_width),
    )


def solution(mesh):
    in_specs = (
        P(("dp", "ctx"), None),
        P(("dp", "ctx"), None),
        P(("dp", "ctx"), None),
        P(("dp", "ctx"), None),
        P("dp", None),
    )
    out_specs = (
        P(("dp", "ctx"), None),
        P(("dp", "ctx"), None),
        P(("dp", "ctx"), None),
        P(("dp", "ctx"), None),
    )
    return jax.shard_map(
        on_device, mesh=mesh, in_specs=in_specs, out_specs=out_specs, check_vma=False
    )
```

profile of v0, /device:TPU:0, one launch (start us, length us, event | category | flops | bytes accessed | tf_op | source)
XLA Modules:
  0.0 890.1 jit_solution(17932902530437409785)
XLA Ops:
  7.2 2.9 slice_bitcast_fusion.15
  10.2 1.8 slice_bitcast_fusion.14
  13.0 1.3 collective-permute-start.1
  15.5 1.6 reshape.369
  17.6 1.5 copy.49
  19.3 26.2 %collective-permute-done.1 = bf16[1,2,128,1536]{3,2,1,0:T(8,128)(2,1)} collective-permute-done((bf16[1,2,128,1536]{3,2,1,0:T(8,128)(2,1)}, bf16[1,2,128,1536]{3,2,1,0:T(8,128)(2,1)}, u32[]{:S(2)}, u32[]{:S(2)}) %collective-permute-start.1) | collective-permute-done | bytes 786464 | tf_op jit(solution)/shard_map/ppermute | solution.py:22
  46.7 4.6 collective-permute-start
  52.0 27.7 %collective-permute-done = bf16[1,2,128,1536]{3,2,1,0:T(8,128)(2,1)S(1)} collective-permute-done((bf16[1,2,128,1536]{3,2,1,0:T(8,128)(2,1)S(1)}, bf16[1,2,128,1536]{3,2,1,0:T(8,128)(2,1)S(1)}, u32[]{:S(2)}, u32[]{:S(2)}) %collective-permute-start) | collective-permute-done | bytes 786464 | tf_op jit(solution)/shard_map/ppermute | solution.py:21
  81.1 185.1 %all-reduce.7.cloned.1.call-done = (bf16[1,128,1536]{2,1,0:T(8,128)(2,1)}, bf16[1,128,1536]{2,1,0:T(8,128)(2,1)}, bf16[1,128,1536]{2,1,0:T(8,128)(2,1)}, bf16[1,...) async-done(((bf16[1,128,1536]{2,1,0:T(8,128)(2,1)}, ...) | async-done | bytes 6291472 | tf_op jit(solution)/shard_map/psum | solution.py:29
  273.1 1.6 copy-done.1
  274.7 2.4 gather_fusion.1
  277.1 2.6 gather_fusion.2
  279.8 3.9 pad_maximum_fusion
  283.7 9.4 %reshape.308 = bf16[2,768,12,128]{3,2,1,0:T(8,128)(2,1)} reshape(bf16[2,6,128,1536]{3,2,1,0:T(8,128)(2,1)} %pad_maximum_fusion) | data formatting | bytes 9437184 | tf_op jit(solution)/shard_map/reshape | solution.py:152
  293.1 3.4 pad_maximum_fusion.1
  296.5 9.4 %reshape.309 = bf16[2,768,12,128]{3,2,1,0:T(8,128)(2,1)} reshape(bf16[2,6,128,1536]{3,2,1,0:T(8,128)(2,1)} %pad_maximum_fusion.1) | data formatting | bytes 9437184 | tf_op jit(solution)/shard_map/reshape | solution.py:149
  306.0 8.7 copy.50
  314.7 3.4 fusion.38
  318.1 7.1 fusion.52
  325.2 4.9 fusion.16
  330.1 5.7 convolution_bitcast_fusion
  335.8 6.9 multiply_reduce_fusion
  342.8 7.1 fusion.1
  349.9 3.2 multiply_bitcast_fusion
  353.1 10.0 %copy.54 = f32[2,768,12,128]{3,2,1,0:T(8,128)} copy(f32[2,768,12,128]{3,1,2,0:T(8,128)S(1)} %multiply_bitcast_fusion) | data formatting | bytes 18874368 | tf_op jit(solution)/shard_map/mul | solution.py:52
  363.2 22.5 %reshape.314 = f32[2,6,128,1536]{3,2,1,0:T(8,128)} reshape(f32[2,768,12,128]{3,2,1,0:T(8,128)} %copy.54) | data formatting | bytes 18874368 | tf_op jit(solution)/shard_map/reshape | solution.py:156
  385.7 13.7 %copy.57 = f32[2,768,12,128]{3,2,1,0:T(8,128)} copy(f32[2,768,12,128]{3,1,2,0:T(8,128)} %convolution_bitcast_fusion) | data formatting | bytes 18874368 | tf_op jit(solution)/shard_map/ghqk,gqhd->gkhd/transpose | solution.py:54
  399.4 11.9 %reshape.316 = f32[2,6,128,1536]{3,2,1,0:T(8,128)} reshape(f32[2,768,12,128]{3,2,1,0:T(8,128)} %copy.57) | data formatting | bytes 18874368 | tf_op jit(solution)/shard_map/reshape | solution.py:157
  411.3 2.8 slice-done
  414.1 9.7 %fusion.13 = f32[8,128,1536]{2,0,1:T(8,128)} fusion(f32[2,4,128,1536]{3,2,1,0:T(8,128)S(1)} %slice-done, s32[2,4]{1,0:T(2,128)S(1)} %gather_fusion, pred[2,4]{1,0:T(4,128)(4,1)S(1)} %add_compare_fusion), kind=kOutput, calls=%fused_computation.23 | convolution fusion | flops 150995072 | bytes 12582952 | tf_op jit(solution)/shard_map/gps,gpbc->sbc/dot_general | solution.py:167
  423.8 9.8 %fusion.10 = f32[8,128,1536]{2,0,1:T(8,128)} fusion(f32[2,4,128,1536]{3,2,1,0:T(8,128)S(1)} %slice-done.4, s32[2,4]{1,0:T(2,128)S(1)} %gather_fusion, pred[2,4]{1,0:T(4,128)(4,1)S(1)} %add_compare_fusion), kind=kOutput, calls=%fused_computation.22 | convolution fusion | flops 150995072 | bytes 12582952 | tf_op jit(solution)/shard_map/gps,gpbc->sbc/dot_general | solution.py:164
  434.2 2.5 fusion.49
  436.6 2.8 fusion.50
  440.7 1.5 collective-permute-start.2
  442.3 5.2 fusion.26
  448.7 5.8 collective-permute-start.3
  456.8 1.9 copy.69
  461.0 1.5 slice_bitcast_fusion
  462.6 34.3 %collective-permute-done.2 = f32[1,2,128,1536]{3,2,1,0:T(8,128)} collective-permute-done((f32[1,2,128,1536]{3,2,1,0:T(8,128)}, f32[1,2,128,1536]{3,2,1,0:T(8,128)}, u32[]{:S(2)}, u32[]{:S(2)}) %collective-permute-start.2) | collective-permute-done | bytes 1572896 | tf_op jit(solution)/shard_map/ppermute | solution.py:22
  496.9 2.2 fusion.31
  499.1 29.7 %collective-permute-done.3 = f32[1,2,128,1536]{3,2,1,0:T(8,128)} collective-permute-done((f32[1,2,128,1536]{3,2,1,0:T(8,128)}, f32[1,2,128,1536]{3,2,1,0:T(8,128)}, u32[]{:S(2)}, u32[]{:S(2)}) %collective-permute-start.3) | collective-permute-done | bytes 1572896 | tf_op jit(solution)/shard_map/ppermute | solution.py:21
  528.8 1.8 fusion.28
  530.6 304.4 %all-reduce.5.cloned.1.call-done = (f32[8,128,1536]{2,0,1:T(8,128)}, f32[8,128,1536]{2,0,1:T(8,128)}) async-done(((f32[8,128,1536]{2,0,1:T(8,128)}, f32[8,128,1536]{2,0,1:T(8,128)}), (f32[8,128,1536]{2,0,1:T(8,128)}, f32[8,128,1536]{2,0,1:T(8,128)})) %all-reduce.5.cloned.1.call-update) | async-done | bytes 12582928 | tf_op jit(solution)/shard_map/psum | solution.py:190
  835.1 10.7 %broadcast_multiply_fusion = (f32[8,128,1536]{2,0,1:T(8,128)}, f32[8,128,1536]{2,0,1:T(8,128)}) fusion(f32[8,128,1536]{2,0,1:T(8,128)} %get-tuple-element.57, f32[8]{0:T(128)S(1)} %compare_convert_fusion, f32[8,128,1536]{2,0,1:T(8,128)} %get-tuple-element.56), kind=kLoop, calls=%fused_computation.29 | loop fusion | flops 3145728 | bytes 25165856 | tf_op jit(solution)/shard_map/mul | solution.py:192
  845.7 9.1 %copy.62 = f32[8,128,1536]{2,1,0:T(8,128)} copy(f32[8,128,1536]{2,0,1:T(8,128)} %get-tuple-element.110) | data formatting | bytes 12582912 | tf_op jit(solution)/shard_map/mul | solution.py:192
  854.8 8.6 scatter_fusion.1
  864.4 9.1 %copy.59 = f32[8,128,1536]{2,1,0:T(8,128)} copy(f32[8,128,1536]{2,0,1:T(8,128)} %get-tuple-element.111) | data formatting | bytes 12582912 | tf_op jit(solution)/shard_map/mul | solution.py:191
  873.5 8.4 scatter_fusion
  (110 shorter events, 22.7 us)
Async XLA Ops:
  7.2 3.0 copy-start.3
  7.2 259.0 %all-reduce.7.cloned.1.call-start = ((), (), s32[]{:S(2)}) async-start(), calls=%async_computation.1 | async-start | bytes 12582912 | tf_op jit(solution)/shard_map/psum | solution.py:29
  12.0 2.3 copy-start.18
  12.0 3.5 copy-start.5
  12.0 5.1 copy-start.6
  12.0 823.1 %all-reduce.5.cloned.1.call-start = ((), (), s32[]{:S(2)}) async-start(), calls=%async_computation | async-start | bytes 25165824 | tf_op jit(solution)/shard_map/psum | solution.py:190
  13.0 32.4 %collective-permute-start.1 = (bf16[1,2,128,1536]{3,2,1,0:T(8,128)(2,1)}, bf16[1,2,128,1536]{3,2,1,0:T(8,128)(2,1)}, u32[]{:S(2)}, u32[]{:S(2)}) collective-permute-start(bf16[1,2,128,1536]{3,2,1,0:T(8,128)(2,1)} %maximum_bitcast_fusion.1), channel_id=1, source_target_pairs={{1,0},{2,1},{3,2},{4,3},{5,4},{6,5},{7,6},{8,7},{9,8},{10,9},{11,1... | collective-permute-start | bytes 2359304 | tf_op jit(solution)/shard_map/ppermute | solution.py:22
  46.7 33.1 %collective-permute-start = (bf16[1,2,128,1536]{3,2,1,0:T(8,128)(2,1)S(1)}, bf16[1,2,128,1536]{3,2,1,0:T(8,128)(2,1)S(1)}, u32[]{:S(2)}, u32[]{:S(2)}) collective-permute-start(bf16[1,2,128,1536]{3,2,1,0:T(8,128)(2,1)S(1)} %get-tuple-element.88), channel_id=1, source_target_pairs={{0,1},{1,2},{2,3},{3,4},{4,5},{5,6},{6,7},{7,8},{8,9},{9,10},{10,1... | collective-permute-start | bytes 2359304 | tf_op jit(solution)/shard_map/ppermute | solution.py:21
  266.1 6.5 copy-start.14
  266.1 6.5 copy-start.13
  266.1 6.6 copy-start.12
  266.1 6.6 copy-start.11
  266.1 6.7 copy-start.10
  266.1 6.7 copy-start.9
  266.2 6.7 copy-start.8
  267.3 5.6 copy-start.7
  268.4 4.6 copy-start.15
  268.4 4.6 copy-start.16
  273.1 1.6 copy-start.1
  306.0 8.7 copy-start
  325.2 4.9 copy-start.2
  330.1 12.7 %slice-start.5 = ((s8[9437184]{0:T(1024)(128)(4,1)}), s8[4194304]{0:T(1024)(128)(4,1)S(1)}, s32[]{:S(2)}) async-start(s8[9437184]{0:T(1024)(128)(4,1)} %bitcast.195), calls=%async_computation.7 | async-start | bytes 8388608
  330.1 12.6 %slice-start.6 = ((s8[9437184]{0:T(1024)(128)(4,1)}), s8[4194304]{0:T(1024)(128)(4,1)S(1)}, s32[]{:S(2)}) async-start(s8[9437184]{0:T(1024)(128)(4,1)} %bitcast.195), calls=%async_computation.8 | async-start | bytes 8388608
  335.8 6.9 slice-start.7
  411.3 2.8 slice-start
  414.1 9.7 %slice-start.4 = ((f32[2,6,128,1536]{3,2,1,0:T(8,128)}), f32[2,4,128,1536]{3,2,1,0:T(8,128)S(1)}, s32[]{:S(2)}) async-start(f32[2,6,128,1536]{3,2,1,0:T(8,128)} %reshape.314), calls=%async_computation.6 | async-start | bytes 12582912 | tf_op jit(solution)/shard_map/slice | solution.py:165
  433.5 0.7 copy-start.19
  436.6 17.8 %slice-start.1 = ((s8[9437184]{0:T(1024)(128)(4,1)}), s8[4194304]{0:T(1024)(128)(4,1)S(1)}, s32[]{:S(2)}) async-start(s8[9437184]{0:T(1024)(128)(4,1)} %bitcast.191), calls=%async_computation.3 | async-start | bytes 8388608
  439.5 15.0 %slice-start.2 = ((s8[9437184]{0:T(1024)(128)(4,1)}), s8[4194304]{0:T(1024)(128)(4,1)S(1)}, s32[]{:S(2)}) async-start(s8[9437184]{0:T(1024)(128)(4,1)} %bitcast.191), calls=%async_computation.4 | async-start | bytes 8388608
  440.7 13.8 %slice-start.3 = ((s8[9437184]{0:T(1024)(128)(4,1)}), s8[1048576]{0:T(1024)(128)(4,1)S(1)}, s32[]{:S(2)}) async-start(s8[9437184]{0:T(1024)(128)(4,1)} %bitcast.191), calls=%async_computation.5 | async-start | bytes 2097152
  440.7 56.2 %collective-permute-start.2 = (f32[1,2,128,1536]{3,2,1,0:T(8,128)}, f32[1,2,128,1536]{3,2,1,0:T(8,128)}, u32[]{:S(2)}, u32[]{:S(2)}) collective-permute-start(f32[1,2,128,1536]{3,2,1,0:T(8,128)} %maximum_bitcast_fusion), channel_id=1, source_target_pairs={{1,0},{2,1},{3,2},{4,3},{5,4},{6,5},{7,6},{8,7},{9,8},{10,9},{11,1... | collective-permute-start | bytes 4718600 | tf_op jit(solution)/shard_map/ppermute | solution.py:22
  448.7 80.1 %collective-permute-start.3 = (f32[1,2,128,1536]{3,2,1,0:T(8,128)}, f32[1,2,128,1536]{3,2,1,0:T(8,128)}, u32[]{:S(2)}, u32[]{:S(2)}) collective-permute-start(f32[1,2,128,1536]{3,2,1,0:T(8,128)} %maximum_select_fusion.1), channel_id=1, source_target_pairs={{0,1},{1,2},{2,3},{3,4},{4,5},{5,6},{6,7},{7,8},{8,9},{9,10},{10,1... | collective-permute-start | bytes 4718600 | tf_op jit(solution)/shard_map/ppermute | solution.py:21
  455.7 4.1 copy-start.4
  845.7 9.1 %copy-start.17 = (s32[8]{0:T(128)S(1)}, s32[8]{0:T(128)}, u32[]{:S(2)}) copy-start(s32[8]{0:T(128)} %constant.160) | copy-start | bytes 100
Sparse Core Ops, SparseCore 0:
  15.0 251.0 all-reduce.6
  433.7 401.3 all-reduce.4
where the time goes:
time: 900 us; the launch traced here: 890 us
  waiting for transfers between devices  607 us (67%)
  local copies, waits for them, and re-layouts  138 us (15%)
  other arithmetic  65.8 us (7%)
  matrix products  51 us (6%)
  between operations  15 us (2%)
  starting transfers between devices  13.3 us (1%)
    psum x1, waiting for transfers between devices, on_device(): total_keys, total_values = lax.psum((summary_gk, summary_gv), 'ctx')  304 us
    psum x1, waiting for transfers between devices, from_root(): return lax.psum(kept, axis)  185 us
    ppermute x2, waiting for transfers between devices, extended_2(): after = lax.ppermute(initial, axis, down)  60.5 us
    ppermute x2, waiting for transfers between devices, extended_2(): before = lax.ppermute(last, axis, up)  57.4 us
    reshape x1, local copies, waits for them, and re-layouts, on_device(): grad_key = grad_key.reshape(group_size, kcount, BLK, feat_width)  22.5 us
    reshape x2, local copies, waits for them, and re-layouts, on_device(): group_keys = jnp.concatenate([prev_keys[0:group_size, None], key_blocks[0...  18.1 us
  transfers between devices with their start and end apart: 6, of which 6 were waited for; matrix products, arithmetic and copies ran while one was open for 4% of the time, Pallas kernels for 0%

commit v1 on v0

v1 whole, which is shorter than its diff:
```python
import functools

import jax
import jax.numpy as jnp
from jax import lax
from jax.experimental import pallas as pl
from jax.experimental.pallas import tpu as pltpu
from jax.sharding import PartitionSpec as P

H = 12
HS = 128
BLK = 128
SUMS = 8
PICKS = 4
GRP = 4
HG = H // GRP
WID = HG * HS
HIDDEN = -1e30
MESH = pl.DeviceIdType.MESH


def both(*terms):
    return functools.reduce(jnp.logical_and, terms)


def either(*terms):
    return functools.reduce(jnp.logical_or, terms)


def home(span, groups):
    return jnp.where(span < groups, span, 2 * groups - 1 - span)


def is_summary(span, every):
    return lax.rem(jnp.asarray(span + 1, jnp.int32), jnp.int32(every)) == 0


def needed(span, group, groups, every):
    span = jnp.asarray(span, jnp.int32)
    group = jnp.asarray(group, jnp.int32)
    return both(
        span <= 2 * groups - 2 - group,
        home(span, groups) != group,
        either(is_summary(span, every), span + 1 == group, span + 1 == 2 * groups - 1 - group),
    )


def dot_nt(a, b):
    return lax.dot_general(a, b, (((1,), (1,)), ((), ())), preferred_element_type=jnp.float32)


def dot_tn(a, b):
    return lax.dot_general(a, b, (((0,), (0,)), ((), ())), preferred_element_type=jnp.float32)


def dot_nn(a, b):
    return lax.dot_general(a, b, (((1,), (0,)), ((), ())), preferred_element_type=jnp.float32)


def member_rows(half, k):
    return (k, slice(0, BLK)) if half == 0 else (GRP - 1 - k, slice(BLK, 2 * BLK))


def kernel(
    groups,
    every,
    q_in, k_in, v_in, g_in, bias,
    o_out, dq_out, dk_out, dv_out,
    q_buf, k_buf, v_buf, g_buf, kvs,
    o_buf, dq_buf, dk_buf, dv_buf,
    sacc, gstage, grecv, last_acc, late,
    in_send, in_recv, loc_in, z_send, z_recv, g_send, g_recv, out_send, out_recv, loc_out,
):
    spans = 2 * groups
    slots = spans - 1
    here = lax.axis_index("ctx")
    group = here // GRP
    member = lax.rem(here, GRP)
    scale = HS ** (-0.5)

    barrier = pltpu.get_barrier_semaphore()
    for off in range(1, GRP):
        peer = group * GRP + lax.rem(member + off, GRP)
        pl.semaphore_signal(barrier, inc=1, device_id={"ctx": peer}, device_id_type=MESH)
    for off in range(1, groups):
        peer = lax.rem(group + off, groups) * GRP + member
        pl.semaphore_signal(barrier, inc=1, device_id={"ctx": peer}, device_id_type=MESH)

    ins = (k_in, v_in, q_in, g_in)
    bufs = (k_buf, v_buf, q_buf, g_buf)
    mine = pl.ds(pl.multiple_of(member * WID, WID), WID)
    for a in range(4):
        pltpu.make_async_copy(ins[a].at[:, mine], bufs[a].at[member], loc_in.at[a]).start()
    for s in range(slots):

        @pl.when(both(jnp.logical_not(needed(s, group, groups, every)), group != s))
        def _():
            kvs[s] = jnp.zeros(kvs.shape[1:], kvs.dtype)

    pl.semaphore_wait(barrier, GRP - 1 + groups - 1)

    front = pl.multiple_of(jnp.where(member < 2, BLK, 0), BLK)
    back = pl.multiple_of(BLK - front, BLK)
    plan = ((0, front), (1, front), (0, back), (1, back), (2, None), (3, None))
    for kind, (a, row) in enumerate(plan):
        rows = pl.ds(0, 2 * BLK) if row is None else pl.ds(row, BLK)
        for m in range(GRP):

            @pl.when(member != m)
            def _():
                pltpu.make_async_remote_copy(
                    src_ref=ins[a].at[rows, pl.ds(m * WID, WID)],
                    dst_ref=bufs[a].at[member, rows, :],
                    send_sem=in_send.at[a],
                    recv_sem=in_recv.at[kind, member],
                    device_id={"ctx": group * GRP + m},
                    device_id_type=MESH,
                ).start()

    def arrived(kind):
        a = plan[kind][0]
        for m in range(GRP):
            first = BLK if m < 2 else 0
            if kind < 2:
                rows = pl.ds(first, BLK)
            elif kind < 4:
                rows = pl.ds(BLK - first, BLK)
            else:
                rows = pl.ds(0, 2 * BLK)

            @pl.when(member != m)
            def _():
                ref = bufs[a].at[m, rows, :]
                pltpu.make_async_copy(ref, ref, in_recv.at[kind, m]).wait()

    for a in range(4):
        pltpu.make_async_copy(ins[a].at[:, mine], bufs[a].at[member], loc_in.at[a]).wait()
    arrived(0)
    arrived(1)

    def span_copy(which, kv, p):
        span = group if which == 0 else spans - 1 - group
        m, rows = member_rows(which, GRP - 1)
        slot = jnp.minimum(span, slots - 1)
        return needed(span, p, groups, every), pltpu.make_async_remote_copy(
            src_ref=(k_buf, v_buf)[kv].at[m, rows, :],
            dst_ref=kvs.at[slot, kv],
            send_sem=z_send.at[which, kv, p],
            recv_sem=z_recv.at[slot, kv],
            device_id={"ctx": p * GRP + member},
            device_id_type=MESH,
        )

    for p in range(groups):
        for which in range(2):
            for kv in range(2):
                wanted, copy = span_copy(which, kv, p)

                @pl.when(wanted)
                def _():
                    copy.start()

    kvs[group, 0] = k_buf[GRP - 1, 0:BLK, :]
    kvs[group, 1] = v_buf[GRP - 1, 0:BLK, :]

    for kind in range(2, 6):
        arrived(kind)
    for s in range(slots):

        @pl.when(needed(s, group, groups, every))
        def _():
            for kv in range(2):
                pltpu.make_async_copy(kvs.at[s, kv], kvs.at[s, kv], z_recv.at[s, kv]).wait()

    key_at = lax.broadcasted_iota(jnp.int32, (BLK, BLK), 0)
    query_at = lax.broadcasted_iota(jnp.int32, (BLK, BLK), 1)
    own_bias = jnp.where(key_at <= query_at, 0.0, HIDDEN).astype(jnp.float32)

    def one_span(half, n, h):
        cols = pl.ds(pl.multiple_of(h * HS, HS), HS)
        at = [member_rows(half, k) for k in range(GRP)]
        q = [q_buf[m, r, cols] for m, r in at]
        g = [g_buf[m, r, cols] for m, r in at]
        kb = [k_buf[m, r, cols] for m, r in at]
        vb = [v_buf[m, r, cols] for m, r in at]
        q_all = jnp.concatenate(q, axis=0)
        g_all = jnp.concatenate(g, axis=0)
        k_sum = kvs[0:n, 0, :, cols].reshape(n * BLK, HS)
        v_sum = kvs[0:n, 1, :, cols].reshape(n * BLK, HS)
        k_two = [jnp.concatenate([kb[max(k - 1, 0)], kb[k]], axis=0) for k in range(GRP)]
        v_two = [jnp.concatenate([vb[max(k - 1, 0)], vb[k]], axis=0) for k in range(GRP)]
        lanes = [slice(k * BLK, (k + 1) * BLK) for k in range(GRP)]

        s_sum = dot_nt(k_sum, q_all).reshape(n, BLK, GRP * BLK) * scale
        s_sum = (s_sum + bias[half, 0:n][:, None, :]).reshape(n * BLK, GRP * BLK)
        local = []
        for k in range(GRP):
            before = jnp.full((BLK, BLK), HIDDEN if k == 0 else 0.0, jnp.float32)
            mask = jnp.concatenate([before, own_bias], axis=0)
            local.append(dot_nt(k_two[k], q[k]) * scale + mask)
        s_loc = jnp.concatenate(local, axis=1)
        top = jnp.maximum(
            jnp.max(s_sum, axis=0, keepdims=True), jnp.max(s_loc, axis=0, keepdims=True)
        )
        p_sum = jnp.exp(s_sum - top)
        p_loc = jnp.exp(s_loc - top)
        total = jnp.sum(p_sum, axis=0, keepdims=True) + jnp.sum(p_loc, axis=0, keepdims=True)
        inv = 1.0 / total
        p_sum = p_sum * inv
        p_loc = p_loc * inv
        low_sum = p_sum.astype(jnp.bfloat16)
        low_loc = p_loc.astype(jnp.bfloat16)

        o_t = dot_tn(v_sum, low_sum) + jnp.concatenate(
            [dot_tn(v_two[k], low_loc[:, lanes[k]]) for k in range(GRP)], axis=1
        )
        o_t = o_t.astype(jnp.bfloat16).astype(jnp.float32)
        g_t = jnp.transpose(g_all.astype(jnp.float32))
        delta = jnp.sum(g_t * o_t, axis=0, keepdims=True)
        attended = jnp.transpose(o_t).astype(jnp.bfloat16)

        dp_sum = dot_nt(v_sum, g_all)
        dp_loc = jnp.concatenate([dot_nt(v_two[k], g[k]) for k in range(GRP)], axis=1)
        ds_sum = (p_sum * (dp_sum - delta)).astype(jnp.bfloat16)
        ds_loc = (p_loc * (dp_loc - delta)).astype(jnp.bfloat16)
        dq_t = dot_tn(k_sum, ds_sum) + jnp.concatenate(
            [dot_tn(k_two[k], ds_loc[:, lanes[k]]) for k in range(GRP)], axis=1
        )
        grad_q = (jnp.transpose(dq_t) * scale).astype(jnp.bfloat16)
        for k, (m, r) in enumerate(at):
            o_buf[m, h, r, :] = attended[lanes[k], :]
            dq_buf[m, h, r, :] = grad_q[lanes[k], :]

        dk_sum = (dot_nn(ds_sum, q_all) * scale).reshape(n, BLK, HS)
        dv_sum = dot_nn(low_sum, g_all).reshape(n, BLK, HS)
        dk_two = [dot_nn(ds_loc[:, lanes[k]], q[k]) * scale for k in range(GRP)]
        dv_two = [dot_nn(low_loc[:, lanes[k]], g[k]) for k in range(GRP)]
        for two, buf, kv in ((dk_two, dk_buf, 0), (dv_two, dv_buf, 1)):
            for k, (m, r) in enumerate(at):
                if k < GRP - 1:
                    buf[m, h, r, :] = (two[k][BLK:] + two[k + 1][:BLK]).astype(jnp.bfloat16)
                else:
                    last_acc[half, h, kv] = two[k][BLK:]
        return dk_sum, dv_sum

    outs = (o_out, dq_out, dk_out, dv_out)
    obufs = (o_buf, dq_buf, dk_buf, dv_buf)

    def grad_copy(s, h):
        return pltpu.make_async_remote_copy(
            src_ref=gstage.at[s, h],
            dst_ref=grecv.at[0 if s < groups else 1, group, h],
            send_sem=g_send.at[s, h],
            recv_sem=g_recv.at[0 if s < groups else 1, group, h],
            device_id={"ctx": (s if s < groups else spans - 1 - s) * GRP + member},
            device_id_type=MESH,
        )

    def send_out(a, src, rows, m, h):
        cols = pl.ds(pl.multiple_of((member * HG + h) * HS, HS), HS)

        @pl.when(member != m)
        def _():
            pltpu.make_async_remote_copy(
                src_ref=src,
                dst_ref=outs[a].at[rows, cols],
                send_sem=out_send.at[a],
                recv_sem=out_recv.at[a],
                device_id={"ctx": group * GRP + m},
                device_id_type=MESH,
            ).start()

        @pl.when(member == m)
        def _():
            pltpu.make_async_copy(src, outs[a].at[rows, cols], loc_out.at[a]).start()

    def one_head(h, carry):
        n_low = groups - 1
        dk_sum, dv_sum = one_span(0, n_low, h)
        sacc[0:n_low, 0] = dk_sum
        sacc[0:n_low, 1] = dv_sum
        dk_sum, dv_sum = one_span(1, slots, h)
        sacc[0:n_low, 0] += dk_sum[:n_low]
        sacc[0:n_low, 1] += dv_sum[:n_low]
        sacc[n_low:slots, 0] = dk_sum[n_low:]
        sacc[n_low:slots, 1] = dv_sum[n_low:]
        for s in range(slots):

            @pl.when(needed(s, group, groups, every))
            def _():
                gstage[s, h] = sacc[s].astype(jnp.bfloat16)
                grad_copy(s, h).start()

        last_acc[0, h] += sacc[group]
        for a in range(4):
            for m in range(GRP):
                if a < 2 or m in (1, 2):
                    rows = pl.ds(0, 2 * BLK)
                else:
                    rows = pl.ds(0 if m == 0 else BLK, BLK)
                send_out(a, obufs[a].at[m, h, rows, :], rows, m, h)
        return carry

    lax.fori_loop(0, HG, one_head, 0)

    def finish_head(h, carry):
        for which in range(2):
            span = group if which == 0 else spans - 1 - group
            for p in range(groups):

                @pl.when(needed(span, p, groups, every))
                def _():
                    ref = grecv.at[which, p, h]
                    pltpu.make_async_copy(ref, ref, g_recv.at[which, p, h]).wait()
                    last_acc[which, h] += grecv[which, p, h].astype(jnp.float32)

            late[which, h] = last_acc[which, h].astype(jnp.bfloat16)
            m = GRP - 1 if which == 0 else 0
            rows = pl.ds(which * BLK, BLK)
            for kv in range(2):
                send_out(2 + kv, late.at[which, h, kv], rows, m, h)
        return carry

    lax.fori_loop(0, HG, finish_head, 0)

    for a in range(4):
        away = ins[a].at[:, pl.ds(0, (GRP - 1) * WID)]
        pltpu.make_async_copy(away, away, in_send.at[a]).wait()
    for p in range(groups):
        for which in range(2):
            for kv in range(2):
                wanted, copy = span_copy(which, kv, p)

                @pl.when(wanted)
                def _():
                    copy.wait_send()

    for s in range(slots):

        @pl.when(needed(s, group, groups, every))
        def _():
            for h in range(HG):
                grad_copy(s, h).wait_send()

    for a in range(4):
        own = outs[a].at[:, pl.ds(0, WID)]
        away = outs[a].at[:, pl.ds(0, (GRP - 1) * WID)]
        pltpu.make_async_copy(own, own, loc_out.at[a]).wait()
        pltpu.make_async_copy(away, away, out_send.at[a]).wait()
        pltpu.make_async_copy(away, away, out_recv.at[a]).wait()


def on_device(queries, keys, values, grad_out, summary_lists):
    rows, width = queries.shape
    groups = lax.axis_size("ctx") // GRP
    every = groups * GRP * 2 // SUMS // GRP
    slots = 2 * groups - 1
    group = lax.axis_index("ctx") // GRP

    first = jnp.stack([group, 2 * groups - 1 - group]) * GRP
    blocks = first[:, None] + jnp.arange(GRP, dtype=jnp.int32)
    spans = jnp.arange(slots, dtype=jnp.int32)
    ends = spans * GRP + GRP - 1
    number = jnp.where((spans + 1) % every == 0, (spans + 1) // every - 1, -1)
    picks = summary_lists[blocks]
    picked = jnp.any(picks[:, None, :, :] == number[None, :, None, None], axis=-1)
    now = blocks[:, None, :]
    then = ends[None, :, None]
    seen = (then == now - 1) | (picked & (then < now - 1))
    bias = jnp.repeat(jnp.where(seen, 0.0, HIDDEN).astype(jnp.float32), BLK, axis=-1)

    bf16, f32 = jnp.bfloat16, jnp.float32
    dma = pltpu.SemaphoreType.DMA
    anywhere = pl.BlockSpec(memory_space=pl.ANY)
    return pl.pallas_call(
        functools.partial(kernel, groups, every),
        out_shape=[jax.ShapeDtypeStruct((rows, width), bf16)] * 4,
        in_specs=[anywhere] * 4 + [pl.BlockSpec(memory_space=pltpu.VMEM)],
        out_specs=[anywhere] * 4,
        scratch_shapes=[pltpu.VMEM((GRP, rows, WID), bf16)] * 4
        + [pltpu.VMEM((slots, 2, BLK, WID), bf16)]
        + [pltpu.VMEM((GRP, HG, rows, HS), bf16)] * 4
        + [
            pltpu.VMEM((slots, 2, BLK, HS), f32),
            pltpu.VMEM((slots, HG, 2, BLK, HS), bf16),
            pltpu.VMEM((2, groups, HG, 2, BLK, HS), bf16),
            pltpu.VMEM((2, HG, 2, BLK, HS), f32),
            pltpu.VMEM((2, HG, 2, BLK, HS), bf16),
            dma((4,)),
            dma((6, GRP)),
            dma((4,)),
            dma((2, 2, groups)),
            dma((slots, 2)),
            dma((slots, HG)),
            dma((2, groups, HG)),
            dma((4,)),
            dma((4,)),
            dma((4,)),
        ],
        compiler_params=pltpu.CompilerParams(
            collective_id=0, has_side_effects=True, vmem_limit_bytes=56 * 1024 * 1024
        ),
        cost_estimate=pl.CostEstimate(
            flops=6 * 10**9, bytes_accessed=8 * 10**6, transcendentals=3 * 10**6
        ),
    )(queries, keys, values, grad_out, bias)


def solution(mesh):
    rows = P(("dp", "ctx"), None)
    return jax.shard_map(
        on_device,
        mesh=mesh,
        in_specs=(rows, rows, rows, rows, P("dp", None)),
        out_specs=(rows, rows, rows, rows),
        check_vma=False,
    )
```

time: 900 us -> 105 us (0.12)
  the two profiles are of different devices: /device:TPU:0 before, /device:TPU:8 now
where the time goes in v1:
time: 105 us
  Pallas kernels  95.6 us (91%)
  local copies, waits for them, and re-layouts  8.09 us (8%)
    pallas_call x1, Pallas kernels, on_device(): pl.pallas_call(functools.partial(kernel, groups, every), out_shape=[jax.S...  95.6 us
    unnamed x13, local copies, waits for them, and re-layouts  6.61 us

profile of v1, /device:TPU:8, one launch (start us, length us, event | category | flops | bytes accessed | tf_op | source)
XLA Modules:
  0.0 104.7 jit_solution(11748789939138316992)
XLA Ops:
  0.6 0.1 add_multiply_fusion
  0.7 0.1 compare_select_fusion
  0.8 0.1 reshape.99
  0.9 0.1 add_add_fusion
  1.0 0.0 copy-start.3
  1.0 0.7 copy-done.3
  1.6 0.1 copy.16
  1.7 0.6 gather_fusion
  2.3 0.1 fusion
  2.4 0.1 or_select_fusion
  2.5 0.1 copy.19
  2.6 0.1 broadcast_in_dim.22
  2.7 0.6 copy.20.bias
  3.3 95.6 %shard_map.84 = (bf16[256,1536]{1,0:T(8,128)(2,1)}, bf16[256,1536]{1,0:T(8,128)(2,1)}, bf16[256,1536]{1,0:T(8,128)(2,1)}, bf16[256,1536]{1,0:T(8,128)(2,1)}) custom-call(bf16[256,1536]{1,0:T(8,128)(2,1)} %q_in.1, bf16[256,1536]{1,0:T(8,128)(2,1)} %k_in.1, bf16[256,1536]{1,0:T(8,128)(2,1)} %v_in.1, bf16[256,1536]{1,0:T(8,128)(2,1)} %g_in.1, ...), custom_call_target="tpu_custom_call" | custom-call | flops 6000000000 | bytes 8000000 | tf_op jit(solution)/shard_map/pallas_call | solution.py:375
  98.9 0.0 copy-start.2
  98.9 2.1 %copy.26 = bf16[256,1536]{1,0:T(8,128)(2,1)} copy(bf16[256,1536]{1,0:T(8,128)(2,1)} %get-tuple-element.8) | data formatting | bytes 1572864
  101.0 0.0 copy-done.2
  101.0 0.0 copy-start.1
  101.0 0.9 copy.27
  101.9 0.5 copy-done.1
  102.4 0.0 copy-start
  102.4 0.9 copy.28
  103.3 0.5 copy-done
  103.8 0.9 copy.29
  (3 shorter events, 0.0 us)
Async XLA Ops:
  1.0 0.7 copy-start.3
  98.9 2.1 %copy-start.2 = (bf16[256,1536]{1,0:T(8,128)(2,1)S(1)}, bf16[256,1536]{1,0:T(8,128)(2,1)}, u32[]{:S(2)}) copy-start(bf16[256,1536]{1,0:T(8,128)(2,1)} %get-tuple-element.9) | copy-start | bytes 2359300
  101.0 1.4 %copy-start.1 = (bf16[256,1536]{1,0:T(8,128)(2,1)S(1)}, bf16[256,1536]{1,0:T(8,128)(2,1)}, u32[]{:S(2)}) copy-start(bf16[256,1536]{1,0:T(8,128)(2,1)} %get-tuple-element.10) | copy-start | bytes 2359300
  102.4 1.4 %copy-start = (bf16[256,1536]{1,0:T(8,128)(2,1)S(1)}, bf16[256,1536]{1,0:T(8,128)(2,1)}, u32[]{:S(2)}) copy-start(bf16[256,1536]{1,0:T(8,128)(2,1)} %get-tuple-element.11) | copy-start | bytes 2359300

commit v2 on v1

--- a/solution.py
+++ b/solution.py
@@ -66,10 +66,11 @@
     every,
     q_in, k_in, v_in, g_in, bias,
     o_out, dq_out, dk_out, dv_out,
-    q_buf, k_buf, v_buf, g_buf, kvs,
+    kv_buf, qg_buf, kvs,
     o_buf, dq_buf, dk_buf, dv_buf,
     sacc, gstage, grecv, last_acc, late,
-    in_send, in_recv, loc_in, z_send, z_recv, g_send, g_recv, out_send, out_recv, loc_out,
+    in_send, first_recv, rest_recv, qg_recv, loc_kv, loc_qg,
+    z_send, z_recv, g_send, g_recv, out_send, out_recv, loc_out,
 ):
     spans = 2 * groups
     slots = spans - 1
@@ -86,11 +87,19 @@
         peer = lax.rem(group + off, groups) * GRP + member
         pl.semaphore_signal(barrier, inc=1, device_id={"ctx": peer}, device_id_type=MESH)
 
-    ins = (k_in, v_in, q_in, g_in)
-    bufs = (k_buf, v_buf, q_buf, g_buf)
-    mine = pl.ds(pl.multiple_of(member * WID, WID), WID)
-    for a in range(4):
-        pltpu.make_async_copy(ins[a].at[:, mine], bufs[a].at[member], loc_in.at[a]).start()
+    def head_cols(m, h):
+        return pl.ds(pl.multiple_of((m * HG + h) * HS, HS), HS)
+
+    for h in range(HG):
+        cols = head_cols(member, h)
+        for half in range(2):
+            rows = pl.ds(half * BLK, BLK)
+            for kv, ref in enumerate((k_in, v_in)):
+                pltpu.make_async_copy(
+                    ref.at[rows, cols], kv_buf.at[member, h, half, kv], loc_kv.at[h]
+                ).start()
+        for i, ref in enumerate((q_in, g_in)):
+            pltpu.make_async_copy(ref.at[:, cols], qg_buf.at[member, h, i], loc_qg.at[h]).start()
     for s in range(slots):
 
         @pl.when(both(jnp.logical_not(needed(s, group, groups, every)), group != s))
@@ -99,94 +108,117 @@
 
     pl.semaphore_wait(barrier, GRP - 1 + groups - 1)
 
-    front = pl.multiple_of(jnp.where(member < 2, BLK, 0), BLK)
-    back = pl.multiple_of(BLK - front, BLK)
-    plan = ((0, front), (1, front), (0, back), (1, back), (2, None), (3, None))
-    for kind, (a, row) in enumerate(plan):
-        rows = pl.ds(0, 2 * BLK) if row is None else pl.ds(row, BLK)
+    front = jnp.where(member < 2, 1, 0)
+
+    def send_kv(h, half, recv):
+        rows = pl.ds(pl.multiple_of(half * BLK, BLK), BLK)
         for m in range(GRP):
 
             @pl.when(member != m)
             def _():
-                pltpu.make_async_remote_copy(
-                    src_ref=ins[a].at[rows, pl.ds(m * WID, WID)],
-                    dst_ref=bufs[a].at[member, rows, :],
-                    send_sem=in_send.at[a],
-                    recv_sem=in_recv.at[kind, member],
-                    device_id={"ctx": group * GRP + m},
-                    device_id_type=MESH,
-                ).start()
-
-    def arrived(kind):
-        a = plan[kind][0]
+                for kv, ref in enumerate((k_in, v_in)):
+                    pltpu.make_async_remote_copy(
+                        src_ref=ref.at[rows, head_cols(m, h)],
+                        dst_ref=kv_buf.at[member, h, half, kv],
+                        send_sem=in_send.at[kv],
+                        recv_sem=recv.at[h, member],
+                        device_id={"ctx": group * GRP + m},
+                        device_id_type=MESH,
+                    ).start()
+
+    def send_qg(h):
         for m in range(GRP):
-            first = BLK if m < 2 else 0
-            if kind < 2:
-                rows = pl.ds(first, BLK)
-            elif kind < 4:
-                rows = pl.ds(BLK - first, BLK)
-            else:
-                rows = pl.ds(0, 2 * BLK)
 
             @pl.when(member != m)
             def _():
-                ref = bufs[a].at[m, rows, :]
-                pltpu.make_async_copy(ref, ref, in_recv.at[kind, m]).wait()
-
-    for a in range(4):
-        pltpu.make_async_copy(ins[a].at[:, mine], bufs[a].at[member], loc_in.at[a]).wait()
-    arrived(0)
-    arrived(1)
-
-    def span_copy(which, kv, p):
+                for i, ref in enumerate((q_in, g_in)):
+                    pltpu.make_async_remote_copy(
+                        src_ref=ref.at[:, head_cols(m, h)],
+                        dst_ref=qg_buf.at[member, h, i],
+                        send_sem=in_send.at[2 + i],
+                        recv_sem=qg_recv.at[h, member],
+                        device_id={"ctx": group * GRP + m},
+                        device_id_type=MESH,
+                    ).start()
+
+    send_kv(0, front, first_recv)
+    send_kv(1, front, first_recv)
+    send_kv(0, 1 - front, rest_recv)
+    send_qg(0)
+    for h in range(1, HG):
+        if h + 1 < HG:
+            send_kv(h + 1, front, first_recv)
+        send_kv(h, 1 - front, rest_recv)
+        send_qg(h)
+
+    def span_copy(which, p, h):
         span = group if which == 0 else spans - 1 - group
-        m, rows = member_rows(which, GRP - 1)
+        m = GRP - 1 if which == 0 else 0
         slot = jnp.minimum(span, slots - 1)
         return needed(span, p, groups, every), pltpu.make_async_remote_copy(
-            src_ref=(k_buf, v_buf)[kv].at[m, rows, :],
-            dst_ref=kvs.at[slot, kv],
-            send_sem=z_send.at[which, kv, p],
-            recv_sem=z_recv.at[slot, kv],
+            src_ref=kv_buf.at[m, h, which],
+            dst_ref=kvs.at[slot, h],
+            send_sem=z_send.at[which, p, h],
+            recv_sem=z_recv.at[slot, h],
             device_id={"ctx": p * GRP + member},
             device_id_type=MESH,
         )
 
-    for p in range(groups):
-        for which in range(2):
-            for kv in range(2):
-                wanted, copy = span_copy(which, kv, p)
+    def spread(h):
+        mine = kv_buf.at[member, h]
+        pltpu.make_async_copy(mine, mine, loc_kv.at[h]).wait()
+        for m in range(GRP):
+
+            @pl.when(member != m)
+            def _():
+                ref = kv_buf.at[m, h, 1 if m < 2 else 0]
+                pltpu.make_async_copy(ref, ref, first_recv.at[h, m]).wait()
+
+        for p in range(groups):
+            for which in range(2):
+                wanted, copy = span_copy(which, p, h)
 
                 @pl.when(wanted)
                 def _():
                     copy.start()
 
-    kvs[group, 0] = k_buf[GRP - 1, 0:BLK, :]
-    kvs[group, 1] = v_buf[GRP - 1, 0:BLK, :]
-
-    for kind in range(2, 6):
-        arrived(kind)
-    for s in range(slots):
-
-        @pl.when(needed(s, group, groups, every))
-        def _():
-            for kv in range(2):
-                pltpu.make_async_copy(kvs.at[s, kv], kvs.at[s, kv], z_recv.at[s, kv]).wait()
+        kvs[group, h] = kv_buf[GRP - 1, h, 0]
+
+    def gather(h):
+        mine = qg_buf.at[member, h]
+        pltpu.make_async_copy(mine, mine, loc_qg.at[h]).wait()
+        for m in range(GRP):
+
+            @pl.when(member != m)
+            def _():
+                ref = kv_buf.at[m, h, 0 if m < 2 else 1]
+                pltpu.make_async_copy(ref, ref, rest_recv.at[h, m]).wait()
+                ref = qg_buf.at[m, h]
+                pltpu.make_async_copy(ref, ref, qg_recv.at[h, m]).wait()
+
+        for s in range(slots):
+
+            @pl.when(needed(s, group, groups, every))
+            def _():
+                pltpu.make_async_copy(kvs.at[s, h], kvs.at[s, h], z_recv.at[s, h]).wait()
+
+    spread(0)
+    spread(1)
 
     key_at = lax.broadcasted_iota(jnp.int32, (BLK, BLK), 0)
     query_at = lax.broadcasted_iota(jnp.int32, (BLK, BLK), 1)
     own_bias = jnp.where(key_at <= query_at, 0.0, HIDDEN).astype(jnp.float32)
 
     def one_span(half, n, h):
-        cols = pl.ds(pl.multiple_of(h * HS, HS), HS)
         at = [member_rows(half, k) for k in range(GRP)]
-        q = [q_buf[m, r, cols] for m, r in at]
-        g = [g_buf[m, r, cols] for m, r in at]
-        kb = [k_buf[m, r, cols] for m, r in at]
-        vb = [v_buf[m, r, cols] for m, r in at]
+        q = [qg_buf[m, h, 0, r, :] for m, r in at]
+        g = [qg_buf[m, h, 1, r, :] for m, r in at]
+        kb = [kv_buf[m, h, half, 0] for m, r in at]
+        vb = [kv_buf[m, h, half, 1] for m, r in at]
         q_all = jnp.concatenate(q, axis=0)
         g_all = jnp.concatenate(g, axis=0)
-        k_sum = kvs[0:n, 0, :, cols].reshape(n * BLK, HS)
-        v_sum = kvs[0:n, 1, :, cols].reshape(n * BLK, HS)
+        k_sum = kvs[0:n, h, 0].reshape(n * BLK, HS)
+        v_sum = kvs[0:n, h, 1].reshape(n * BLK, HS)
         k_two = [jnp.concatenate([kb[max(k - 1, 0)], kb[k]], axis=0) for k in range(GRP)]
         v_two = [jnp.concatenate([vb[max(k - 1, 0)], vb[k]], axis=0) for k in range(GRP)]
         lanes = [slice(k * BLK, (k + 1) * BLK) for k in range(GRP)]
@@ -274,8 +306,26 @@
         def _():
             pltpu.make_async_copy(src, outs[a].at[rows, cols], loc_out.at[a]).start()
 
+    def finish_head(h):
+        for which in range(2):
+            span = group if which == 0 else spans - 1 - group
+            for p in range(groups):
+
+                @pl.when(needed(span, p, groups, every))
+                def _():
+                    ref = grecv.at[which, p, h]
+                    pltpu.make_async_copy(ref, ref, g_recv.at[which, p, h]).wait()
+                    last_acc[which, h] += grecv[which, p, h].astype(jnp.float32)
+
+            late[which, h] = last_acc[which, h].astype(jnp.bfloat16)
+            m = GRP - 1 if which == 0 else 0
+            rows = pl.ds(which * BLK, BLK)
+            for kv in range(2):
+                send_out(2 + kv, late.at[which, h, kv], rows, m, h)
+
     def one_head(h, carry):
         n_low = groups - 1
+        gather(h)
         dk_sum, dv_sum = one_span(0, n_low, h)
         sacc[0:n_low, 0] = dk_sum
         sacc[0:n_low, 1] = dv_sum
@@ -299,37 +349,28 @@
                 else:
                     rows = pl.ds(0 if m == 0 else BLK, BLK)
                 send_out(a, obufs[a].at[m, h, rows, :], rows, m, h)
+
+        @pl.when(h + 2 < HG)
+        def _():
+            spread(h + 2)
+
+        @pl.when(h > 0)
+        def _():
+            finish_head(h - 1)
+
         return carry
 
     lax.fori_loop(0, HG, one_head, 0)
 
-    def finish_head(h, carry):
-        for which in range(2):
-            span = group if which == 0 else spans - 1 - group
-            for p in range(groups):
-
-                @pl.when(needed(span, p, groups, every))
-                def _():
-                    ref = grecv.at[which, p, h]
-                    pltpu.make_async_copy(ref, ref, g_recv.at[which, p, h]).wait()
-                    last_acc[which, h] += grecv[which, p, h].astype(jnp.float32)
-
-            late[which, h] = last_acc[which, h].astype(jnp.bfloat16)
-            m = GRP - 1 if which == 0 else 0
-            rows = pl.ds(which * BLK, BLK)
-            for kv in range(2):
-                send_out(2 + kv, late.at[which, h, kv], rows, m, h)
-        return carry
-
-    lax.fori_loop(0, HG, finish_head, 0)
+    finish_head(HG - 1)
 
     for a in range(4):
-        away = ins[a].at[:, pl.ds(0, (GRP - 1) * WID)]
+        away = (k_in, v_in, q_in, g_in)[a].at[:, pl.ds(0, (GRP - 1) * WID)]
         pltpu.make_async_copy(away, away, in_send.at[a]).wait()
     for p in range(groups):
         for which in range(2):
-            for kv in range(2):
-                wanted, copy = span_copy(which, kv, p)
+            for h in range(HG):
+                wanted, copy = span_copy(which, p, h)
 
                 @pl.when(wanted)
                 def _():
@@ -377,8 +418,11 @@
         out_shape=[jax.ShapeDtypeStruct((rows, width), bf16)] * 4,
         in_specs=[anywhere] * 4 + [pl.BlockSpec(memory_space=pltpu.VMEM)],
         out_specs=[anywhere] * 4,
-        scratch_shapes=[pltpu.VMEM((GRP, rows, WID), bf16)] * 4
-        + [pltpu.VMEM((slots, 2, BLK, WID), bf16)]
+        scratch_shapes=[
+            pltpu.VMEM((GRP, HG, 2, 2, BLK, HS), bf16),
+            pltpu.VMEM((GRP, HG, 2, rows, HS), bf16),
+            pltpu.VMEM((slots, HG, 2, BLK, HS), bf16),
+        ]
         + [pltpu.VMEM((GRP, HG, rows, HS), bf16)] * 4
         + [
             pltpu.VMEM((slots, 2, BLK, HS), f32),
@@ -387,10 +431,13 @@
             pltpu.VMEM((2, HG, 2, BLK, HS), f32),
             pltpu.VMEM((2, HG, 2, BLK, HS), bf16),
             dma((4,)),
-            dma((6, GRP)),
-            dma((4,)),
-            dma((2, 2, groups)),
-            dma((slots, 2)),
+            dma((HG, GRP)),
+            dma((HG, GRP)),
+            dma((HG, GRP)),
+            dma((HG,)),
+            dma((HG,)),
+            dma((2, groups, HG)),
+            dma((slots, HG)),
             dma((slots, HG)),
             dma((2, groups, HG)),
             dma((4,)),

time: 105 us -> 87.2 us (0.83)
  the two profiles are of different devices: /device:TPU:8 before, /device:TPU:0 now
where the time goes in v2:
time: 87.2 us; the launch traced here: 86.9 us
  Pallas kernels  77.7 us (89%)
  local copies, waits for them, and re-layouts  8.09 us (9%)
    pallas_call x1, Pallas kernels, on_device(): pl.pallas_call(functools.partial(kernel, groups, every), out_shape=[jax.S...  77.7 us
    unnamed x13, local copies, waits for them, and re-layouts  6.61 us

profile of v2, /device:TPU:0, one launch (start us, length us, event | category | flops | bytes accessed | tf_op | source)
XLA Modules:
  0.0 86.9 jit_solution(17000212739295452731)
XLA Ops:
  0.6 0.1 add_multiply_fusion
  0.7 0.1 compare_select_fusion
  0.8 0.1 reshape.99
  0.9 0.1 add_add_fusion
  1.0 0.0 copy-start.3
  1.0 0.7 copy-done.3
  1.6 0.1 copy.16
  1.7 0.6 gather_fusion
  2.3 0.1 fusion
  2.4 0.1 or_select_fusion
  2.5 0.1 copy.19
  2.6 0.1 broadcast_in_dim.22
  2.7 0.6 copy.20.bias
  3.3 77.7 %shard_map.84 = (bf16[256,1536]{1,0:T(8,128)(2,1)}, bf16[256,1536]{1,0:T(8,128)(2,1)}, bf16[256,1536]{1,0:T(8,128)(2,1)}, bf16[256,1536]{1,0:T(8,128)(2,1)}) custom-call(bf16[256,1536]{1,0:T(8,128)(2,1)} %q_in.1, bf16[256,1536]{1,0:T(8,128)(2,1)} %k_in.1, bf16[256,1536]{1,0:T(8,128)(2,1)} %v_in.1, bf16[256,1536]{1,0:T(8,128)(2,1)} %g_in.1, ...), custom_call_target="tpu_custom_call" | custom-call | flops 6000000000 | bytes 8000000 | tf_op jit(solution)/shard_map/pallas_call | solution.py:416
  81.0 0.0 copy-start.2
  81.0 2.1 %copy.26 = bf16[256,1536]{1,0:T(8,128)(2,1)} copy(bf16[256,1536]{1,0:T(8,128)(2,1)} %get-tuple-element.8) | data formatting | bytes 1572864
  83.2 0.0 copy-done.2
  83.2 0.0 copy-start.1
  83.2 0.9 %copy.27 = bf16[256,1536]{1,0:T(8,128)(2,1)} copy(bf16[256,1536]{1,0:T(8,128)(2,1)S(1)} %copy-done.2) | data formatting | bytes 1572864
  84.0 0.5 copy-done.1
  84.6 0.0 copy-start
  84.6 0.9 %copy.28 = bf16[256,1536]{1,0:T(8,128)(2,1)} copy(bf16[256,1536]{1,0:T(8,128)(2,1)S(1)} %copy-done.1) | data formatting | bytes 1572864
  85.5 0.5 copy-done
  86.0 0.9 %copy.29 = bf16[256,1536]{1,0:T(8,128)(2,1)} copy(bf16[256,1536]{1,0:T(8,128)(2,1)S(1)} %copy-done) | data formatting | bytes 1572864
  (3 shorter events, 0.0 us)
Async XLA Ops:
  1.0 0.7 copy-start.3
  81.0 2.1 %copy-start.2 = (bf16[256,1536]{1,0:T(8,128)(2,1)S(1)}, bf16[256,1536]{1,0:T(8,128)(2,1)}, u32[]{:S(2)}) copy-start(bf16[256,1536]{1,0:T(8,128)(2,1)} %get-tuple-element.9) | copy-start | bytes 2359300
  83.2 1.4 %copy-start.1 = (bf16[256,1536]{1,0:T(8,128)(2,1)S(1)}, bf16[256,1536]{1,0:T(8,128)(2,1)}, u32[]{:S(2)}) copy-start(bf16[256,1536]{1,0:T(8,128)(2,1)} %get-tuple-element.10) | copy-start | bytes 2359300
  84.6 1.4 %copy-start = (bf16[256,1536]{1,0:T(8,128)(2,1)S(1)}, bf16[256,1536]{1,0:T(8,128)(2,1)}, u32[]{:S(2)}) copy-start(bf16[256,1536]{1,0:T(8,128)(2,1)} %get-tuple-element.11) | copy-start | bytes 2359300

commit v3 on v2

--- a/solution.py
+++ b/solution.py
@@ -12,10 +12,12 @@
 BLK = 128
 SUMS = 8
 PICKS = 4
+PIECES = 4
 GRP = 4
 HG = H // GRP
 WID = HG * HS
 HIDDEN = -1e30
+LOG2_E = 1.4426950408889634
 MESH = pl.DeviceIdType.MESH
 
 
@@ -64,12 +66,12 @@
 def kernel(
     groups,
     every,
-    q_in, k_in, v_in, g_in, bias,
+    q_in, k_in, v_in, g_in, lists,
     o_out, dq_out, dk_out, dv_out,
     kv_buf, qg_buf, kvs,
     o_buf, dq_buf, dk_buf, dv_buf,
     sacc, gstage, grecv, last_acc, late,
-    in_send, first_recv, rest_recv, qg_recv, loc_kv, loc_qg,
+    bias, in_send, first_recv, rest_recv, qg_recv, loc_kv, loc_qg,
     z_send, z_recv, g_send, g_recv, out_send, out_recv, loc_out,
 ):
     spans = 2 * groups
@@ -78,6 +80,7 @@
     group = here // GRP
     member = lax.rem(here, GRP)
     scale = HS ** (-0.5)
+    scale_2 = scale * LOG2_E
 
     barrier = pltpu.get_barrier_semaphore()
     for off in range(1, GRP):
@@ -201,6 +204,19 @@
             @pl.when(needed(s, group, groups, every))
             def _():
                 pltpu.make_async_copy(kvs.at[s, h], kvs.at[s, h], z_recv.at[s, h]).wait()
+
+    for half in range(2):
+        for k in range(GRP):
+            block = (group if half == 0 else spans - 1 - group) * GRP + k
+            picks = [lists[block, i] for i in range(PICKS)]
+            for s in range(slots):
+                end = s * GRP + GRP - 1
+                seen = end == block - 1
+                if (s + 1) % every == 0:
+                    picked = either(*[pick == (s + 1) // every - 1 for pick in picks])
+                    seen = either(seen, both(picked, end < block - 1))
+                row = jnp.full((1, BLK), jnp.where(seen, 0.0, HIDDEN), jnp.float32)
+                bias[half, s, :, k * BLK : (k + 1) * BLK] = row
 
     spread(0)
     spread(1)
@@ -223,19 +239,18 @@
         v_two = [jnp.concatenate([vb[max(k - 1, 0)], vb[k]], axis=0) for k in range(GRP)]
         lanes = [slice(k * BLK, (k + 1) * BLK) for k in range(GRP)]
 
-        s_sum = dot_nt(k_sum, q_all).reshape(n, BLK, GRP * BLK) * scale
-        s_sum = (s_sum + bias[half, 0:n][:, None, :]).reshape(n * BLK, GRP * BLK)
+        s_sum = dot_nt(k_sum, q_all).reshape(n, BLK, GRP * BLK)
         local = []
         for k in range(GRP):
             before = jnp.full((BLK, BLK), HIDDEN if k == 0 else 0.0, jnp.float32)
             mask = jnp.concatenate([before, own_bias], axis=0)
-            local.append(dot_nt(k_two[k], q[k]) * scale + mask)
+            local.append(dot_nt(k_two[k], q[k]) * scale_2 + mask)
         s_loc = jnp.concatenate(local, axis=1)
-        top = jnp.maximum(
-            jnp.max(s_sum, axis=0, keepdims=True), jnp.max(s_loc, axis=0, keepdims=True)
-        )
-        p_sum = jnp.exp(s_sum - top)
-        p_loc = jnp.exp(s_loc - top)
+        hide = bias[half, 0:n]
+        top_sum = jnp.max(s_sum, axis=1, keepdims=True) * scale_2 + hide
+        top = jnp.maximum(jnp.max(top_sum, axis=0), jnp.max(s_loc, axis=0, keepdims=True))
+        p_sum = jnp.exp2(s_sum * scale_2 + (hide - top[None])).reshape(n * BLK, GRP * BLK)
+        p_loc = jnp.exp2(s_loc - top)
         total = jnp.sum(p_sum, axis=0, keepdims=True) + jnp.sum(p_loc, axis=0, keepdims=True)
         inv = 1.0 / total
         p_sum = p_sum * inv
@@ -391,32 +406,36 @@
         pltpu.make_async_copy(away, away, out_recv.at[a]).wait()
 
 
+def place(*refs):
+    sources, targets, sems = refs[:4], refs[4:8], refs[8]
+    step = sources[0].shape[0] // PIECES
+    copies = [
+        pltpu.make_async_copy(
+            sources[a].at[pl.ds(i * step, step)], targets[a].at[pl.ds(i * step, step)], sems.at[a, i]
+        )
+        for a in range(4)
+        for i in range(PIECES)
+    ]
+    for copy in copies:
+        copy.start()
+    for copy in copies:
+        copy.wait()
+
+
 def on_device(queries, keys, values, grad_out, summary_lists):
     rows, width = queries.shape
     groups = lax.axis_size("ctx") // GRP
     every = groups * GRP * 2 // SUMS // GRP
     slots = 2 * groups - 1
-    group = lax.axis_index("ctx") // GRP
-
-    first = jnp.stack([group, 2 * groups - 1 - group]) * GRP
-    blocks = first[:, None] + jnp.arange(GRP, dtype=jnp.int32)
-    spans = jnp.arange(slots, dtype=jnp.int32)
-    ends = spans * GRP + GRP - 1
-    number = jnp.where((spans + 1) % every == 0, (spans + 1) // every - 1, -1)
-    picks = summary_lists[blocks]
-    picked = jnp.any(picks[:, None, :, :] == number[None, :, None, None], axis=-1)
-    now = blocks[:, None, :]
-    then = ends[None, :, None]
-    seen = (then == now - 1) | (picked & (then < now - 1))
-    bias = jnp.repeat(jnp.where(seen, 0.0, HIDDEN).astype(jnp.float32), BLK, axis=-1)
 
     bf16, f32 = jnp.bfloat16, jnp.float32
     dma = pltpu.SemaphoreType.DMA
     anywhere = pl.BlockSpec(memory_space=pl.ANY)
-    return pl.pallas_call(
+    shapes = [jax.ShapeDtypeStruct((rows, width), bf16)] * 4
+    results = pl.pallas_call(
         functools.partial(kernel, groups, every),
-        out_shape=[jax.ShapeDtypeStruct((rows, width), bf16)] * 4,
-        in_specs=[anywhere] * 4 + [pl.BlockSpec(memory_space=pltpu.VMEM)],
+        out_shape=shapes,
+        in_specs=[anywhere] * 4 + [pl.BlockSpec(memory_space=pltpu.SMEM)],
         out_specs=[anywhere] * 4,
         scratch_shapes=[
             pltpu.VMEM((GRP, HG, 2, 2, BLK, HS), bf16),
@@ -430,6 +449,7 @@
             pltpu.VMEM((2, groups, HG, 2, BLK, HS), bf16),
             pltpu.VMEM((2, HG, 2, BLK, HS), f32),
             pltpu.VMEM((2, HG, 2, BLK, HS), bf16),
+            pltpu.VMEM((2, slots, 1, GRP * BLK), f32),
             dma((4,)),
             dma((HG, GRP)),
             dma((HG, GRP)),
@@ -450,7 +470,16 @@
         cost_estimate=pl.CostEstimate(
             flops=6 * 10**9, bytes_accessed=8 * 10**6, transcendentals=3 * 10**6
         ),
-    )(queries, keys, values, grad_out, bias)
+    )(queries, keys, values, grad_out, summary_lists)
+    return pl.pallas_call(
+        place,
+        out_shape=shapes,
+        in_specs=[anywhere] * 4,
+        out_specs=[anywhere] * 4,
+        scratch_shapes=[dma((4, PIECES))],
+        compiler_params=pltpu.CompilerParams(vmem_limit_bytes=60 * 1024 * 1024),
+        cost_estimate=pl.CostEstimate(flops=0, bytes_accessed=6 * 10**6, transcendentals=0),
+    )(*results)
 
 
 def solution(mesh):

time: 87.2 us -> 177 us (2.03)
  Pallas kernels: 77.7 us -> 174 us
  local copies, waits for them, and re-layouts: 8.09 us -> 1.37 us
    pallas_call x1 -> x2, Pallas kernels: 77.7 us -> 174 us  [the longest x1 96.5 us: on_device(): pl.pallas_call(place, out_shape=shapes, in_specs=[anywhere] * 4, out_spec...]
    unnamed x13 -> x1, local copies, waits for them, and re-layouts: 6.61 us -> 1.37 us
where the time goes in v3:
time: 177 us; the launch traced here: 176 us
  Pallas kernels  174 us (98%)
    pallas_call x1, Pallas kernels, on_device(): pl.pallas_call(place, out_shape=shapes, in_specs=[anywhere] * 4, out_spec...  96.5 us
    pallas_call x1, Pallas kernels, on_device(): pl.pallas_call(functools.partial(kernel, groups, every), out_shape=shapes...  77.9 us

profile of v3, /device:TPU:0, one launch (start us, length us, event | category | flops | bytes accessed | tf_op | source)
XLA Modules:
  0.0 176.5 jit_solution(3903719926237161775)
XLA Ops:
  0.6 1.4 copy.9.lists
  2.0 77.9 %shard_map.84 = (bf16[256,1536]{1,0:T(8,128)(2,1)}, bf16[256,1536]{1,0:T(8,128)(2,1)}, bf16[256,1536]{1,0:T(8,128)(2,1)}, bf16[256,1536]{1,0:T(8,128)(2,1)}) custom-call(bf16[256,1536]{1,0:T(8,128)(2,1)} %q_in.1, bf16[256,1536]{1,0:T(8,128)(2,1)} %k_in.1, bf16[256,1536]{1,0:T(8,128)(2,1)} %v_in.1, bf16[256,1536]{1,0:T(8,128)(2,1)} %g_in.1, s32[32,4]{1,0:T(8,128)} %copy.9.lists), custom_call_target="tpu_custom_call" | custom-call | flops 6000000000 | bytes 8000000 | tf_op jit(solution)/shard_map/pallas_call | solution.py:435
  79.9 96.5 %shard_map.85 = (bf16[256,1536]{1,0:T(8,128)(2,1)}, bf16[256,1536]{1,0:T(8,128)(2,1)}, bf16[256,1536]{1,0:T(8,128)(2,1)}, bf16[256,1536]{1,0:T(8,128)(2,1)}) custom-call(bf16[256,1536]{1,0:T(8,128)(2,1)} %get-tuple-element.8.refs_0_, bf16[256,1536]{1,0:T(8,128)(2,1)} %get-tuple-element.9.refs_1_, bf16[256,1536]{1,0:T(8,128)(2,1)} %get-tuple-element.10.refs_2_, ...), custom_call_target="tpu_custom_call" | custom-call | bytes 6000000 | tf_op jit(solution)/shard_map/pallas_call | solution.py:474

commit v4 on v3

--- a/solution.py
+++ b/solution.py
@@ -45,14 +45,6 @@
         home(span, groups) != group,
         either(is_summary(span, every), span + 1 == group, span + 1 == 2 * groups - 1 - group),
     )
-
-
-def dot_nt(a, b):
-    return lax.dot_general(a, b, (((1,), (1,)), ((), ())), preferred_element_type=jnp.float32)
-
-
-def dot_tn(a, b):
-    return lax.dot_general(a, b, (((0,), (0,)), ((), ())), preferred_element_type=jnp.float32)
 
 
 def dot_nn(a, b):
@@ -225,7 +217,7 @@
     query_at = lax.broadcasted_iota(jnp.int32, (BLK, BLK), 1)
     own_bias = jnp.where(key_at <= query_at, 0.0, HIDDEN).astype(jnp.float32)
 
-    def one_span(half, n, h):
+    def one_span(half, n, h, k_sum, v_sum, k_sum_t, v_sum_t):
         at = [member_rows(half, k) for k in range(GRP)]
         q = [qg_buf[m, h, 0, r, :] for m, r in at]
         g = [qg_buf[m, h, 1, r, :] for m, r in at]
@@ -233,18 +225,22 @@
         vb = [kv_buf[m, h, half, 1] for m, r in at]
         q_all = jnp.concatenate(q, axis=0)
         g_all = jnp.concatenate(g, axis=0)
-        k_sum = kvs[0:n, h, 0].reshape(n * BLK, HS)
-        v_sum = kvs[0:n, h, 1].reshape(n * BLK, HS)
+        q_t = jnp.transpose(q_all)
+        g_t = jnp.transpose(g_all)
         k_two = [jnp.concatenate([kb[max(k - 1, 0)], kb[k]], axis=0) for k in range(GRP)]
         v_two = [jnp.concatenate([vb[max(k - 1, 0)], vb[k]], axis=0) for k in range(GRP)]
+        kb_t = [jnp.transpose(block) for block in kb]
+        vb_t = [jnp.transpose(block) for block in vb]
+        k_two_t = [jnp.concatenate([kb_t[max(k - 1, 0)], kb_t[k]], axis=1) for k in range(GRP)]
+        v_two_t = [jnp.concatenate([vb_t[max(k - 1, 0)], vb_t[k]], axis=1) for k in range(GRP)]
         lanes = [slice(k * BLK, (k + 1) * BLK) for k in range(GRP)]
 
-        s_sum = dot_nt(k_sum, q_all).reshape(n, BLK, GRP * BLK)
+        s_sum = dot_nn(k_sum, q_t).reshape(n, BLK, GRP * BLK)
         local = []
         for k in range(GRP):
             before = jnp.full((BLK, BLK), HIDDEN if k == 0 else 0.0, jnp.float32)
             mask = jnp.concatenate([before, own_bias], axis=0)
-            local.append(dot_nt(k_two[k], q[k]) * scale_2 + mask)
+            local.append(dot_nn(k_two[k], q_t[:, lanes[k]]) * scale_2 + mask)
         s_loc = jnp.concatenate(local, axis=1)
         hide = bias[half, 0:n]
         top_sum = jnp.max(s_sum, axis=1, keepdims=True) * scale_2 + hide
@@ -258,22 +254,23 @@
         low_sum = p_sum.astype(jnp.bfloat16)
         low_loc = p_loc.astype(jnp.bfloat16)
 
-        o_t = dot_tn(v_sum, low_sum) + jnp.concatenate(
-            [dot_tn(v_two[k], low_loc[:, lanes[k]]) for k in range(GRP)], axis=1
+        o_t = dot_nn(v_sum_t, low_sum) + jnp.concatenate(
+            [dot_nn(v_two_t[k], low_loc[:, lanes[k]]) for k in range(GRP)], axis=1
         )
-        o_t = o_t.astype(jnp.bfloat16).astype(jnp.float32)
-        g_t = jnp.transpose(g_all.astype(jnp.float32))
-        delta = jnp.sum(g_t * o_t, axis=0, keepdims=True)
-        attended = jnp.transpose(o_t).astype(jnp.bfloat16)
-
-        dp_sum = dot_nt(v_sum, g_all)
-        dp_loc = jnp.concatenate([dot_nt(v_two[k], g[k]) for k in range(GRP)], axis=1)
+        o_t = o_t.astype(jnp.bfloat16)
+        delta = jnp.sum(
+            g_t.astype(jnp.float32) * o_t.astype(jnp.float32), axis=0, keepdims=True
+        )
+        attended = jnp.transpose(o_t)
+
+        dp_sum = dot_nn(v_sum, g_t)
+        dp_loc = jnp.concatenate([dot_nn(v_two[k], g_t[:, lanes[k]]) for k in range(GRP)], axis=1)
         ds_sum = (p_sum * (dp_sum - delta)).astype(jnp.bfloat16)
         ds_loc = (p_loc * (dp_loc - delta)).astype(jnp.bfloat16)
-        dq_t = dot_tn(k_sum, ds_sum) + jnp.concatenate(
-            [dot_tn(k_two[k], ds_loc[:, lanes[k]]) for k in range(GRP)], axis=1
+        dq_t = dot_nn(k_sum_t, ds_sum) + jnp.concatenate(
+            [dot_nn(k_two_t[k], ds_loc[:, lanes[k]]) for k in range(GRP)], axis=1
         )
-        grad_q = (jnp.transpose(dq_t) * scale).astype(jnp.bfloat16)
+        grad_q = jnp.transpose((dq_t * scale).astype(jnp.bfloat16))
         for k, (m, r) in enumerate(at):
             o_buf[m, h, r, :] = attended[lanes[k], :]
             dq_buf[m, h, r, :] = grad_q[lanes[k], :]
@@ -341,21 +338,30 @@
     def one_head(h, carry):
         n_low = groups - 1
         gather(h)
-        dk_sum, dv_sum = one_span(0, n_low, h)
-        sacc[0:n_low, 0] = dk_sum
-        sacc[0:n_low, 1] = dv_sum
-        dk_sum, dv_sum = one_span(1, slots, h)
-        sacc[0:n_low, 0] += dk_sum[:n_low]
-        sacc[0:n_low, 1] += dv_sum[:n_low]
-        sacc[n_low:slots, 0] = dk_sum[n_low:]
-        sacc[n_low:slots, 1] = dv_sum[n_low:]
-        for s in range(slots):
-
-            @pl.when(needed(s, group, groups, every))
-            def _():
-                gstage[s, h] = sacc[s].astype(jnp.bfloat16)
-                grad_copy(s, h).start()
-
+        k_sum = kvs[0:slots, h, 0].reshape(slots * BLK, HS)
+        v_sum = kvs[0:slots, h, 1].reshape(slots * BLK, HS)
+        k_sum_t = jnp.transpose(k_sum)
+        v_sum_t = jnp.transpose(v_sum)
+
+        def ship(first, end):
+            for s in range(first, end):
+
+                @pl.when(needed(s, group, groups, every))
+                def _():
+                    gstage[s, h] = sacc[s].astype(jnp.bfloat16)
+                    grad_copy(s, h).start()
+
+        dk_sum, dv_sum = one_span(1, slots, h, k_sum, v_sum, k_sum_t, v_sum_t)
+        sacc[:, 0] = dk_sum
+        sacc[:, 1] = dv_sum
+        ship(n_low, slots)
+        low = n_low * BLK
+        dk_sum, dv_sum = one_span(
+            0, n_low, h, k_sum[:low], v_sum[:low], k_sum_t[:, :low], v_sum_t[:, :low]
+        )
+        sacc[0:n_low, 0] += dk_sum
+        sacc[0:n_low, 1] += dv_sum
+        ship(0, n_low)
         last_acc[0, h] += sacc[group]
         for a in range(4):
             for m in range(GRP):
@@ -407,19 +413,26 @@
 
 
 def place(*refs):
-    sources, targets, sems = refs[:4], refs[4:8], refs[8]
+    sources, targets, held, arrive, leave = refs[:4], refs[4:8], refs[8], refs[9], refs[10]
     step = sources[0].shape[0] // PIECES
-    copies = [
-        pltpu.make_async_copy(
-            sources[a].at[pl.ds(i * step, step)], targets[a].at[pl.ds(i * step, step)], sems.at[a, i]
-        )
-        for a in range(4)
-        for i in range(PIECES)
-    ]
-    for copy in copies:
-        copy.start()
-    for copy in copies:
-        copy.wait()
+    pairs = []
+    for a in range(4):
+        for i in range(PIECES):
+            rows = pl.ds(i * step, step)
+            mid = held.at[a, rows]
+            pairs.append(
+                (
+                    pltpu.make_async_copy(sources[a].at[rows], mid, arrive.at[a, i]),
+                    pltpu.make_async_copy(mid, targets[a].at[rows], leave.at[a, i]),
+                )
+            )
+    for load, _ in pairs:
+        load.start()
+    for load, store in pairs:
+        load.wait()
+        store.start()
+    for _, store in pairs:
+        store.wait()
 
 
 def on_device(queries, keys, values, grad_out, summary_lists):
@@ -476,7 +489,7 @@
         out_shape=shapes,
         in_specs=[anywhere] * 4,
         out_specs=[anywhere] * 4,
-        scratch_shapes=[dma((4, PIECES))],
+        scratch_shapes=[pltpu.VMEM((4, rows, width), bf16), dma((4, PIECES)), dma((4, PIECES))],
         compiler_params=pltpu.CompilerParams(vmem_limit_bytes=60 * 1024 * 1024),
         cost_estimate=pl.CostEstimate(flops=0, bytes_accessed=6 * 10**6, transcendentals=0),
     )(*results)

time: 177 us -> 83.4 us (0.47)
  Pallas kernels: 174 us -> 81.1 us
    pallas_call x1, Pallas kernels: 96.5 us -> 3.18 us  [on_device(): pl.pallas_call(place, out_shape=shapes, in_specs=[anywhere] * 4, out_spec...]
where the time goes in v4:
time: 83.4 us; the launch traced here: 83.1 us
  Pallas kernels  81.1 us (97%)
  local copies, waits for them, and re-layouts  1.37 us (2%)
    pallas_call x1, Pallas kernels, on_device(): pl.pallas_call(functools.partial(kernel, groups, every), out_shape=shapes...  77.9 us
    pallas_call x1, Pallas kernels, on_device(): pl.pallas_call(place, out_shape=shapes, in_specs=[anywhere] * 4, out_spec...  3.18 us

profile of v4, /device:TPU:0, one launch (start us, length us, event | category | flops | bytes accessed | tf_op | source)
XLA Modules:
  0.0 83.1 jit_solution(2650792753615797269)
XLA Ops:
  0.6 1.4 %copy.9.lists = s32[32,4]{1,0:T(8,128)} copy(s32[32,4]{0,1:T(4,128)} %param.9) | data formatting | bytes 1024 | tf_op args[4]
  2.0 77.9 %shard_map.84 = (bf16[256,1536]{1,0:T(8,128)(2,1)}, bf16[256,1536]{1,0:T(8,128)(2,1)}, bf16[256,1536]{1,0:T(8,128)(2,1)}, bf16[256,1536]{1,0:T(8,128)(2,1)}) custom-call(bf16[256,1536]{1,0:T(8,128)(2,1)} %q_in.1, bf16[256,1536]{1,0:T(8,128)(2,1)} %k_in.1, bf16[256,1536]{1,0:T(8,128)(2,1)} %v_in.1, bf16[256,1536]{1,0:T(8,128)(2,1)} %g_in.1, s32[32,4]{1,0:T(8,128)} %copy.9.lists), custom_call_target="tpu_custom_call" | custom-call | flops 6000000000 | bytes 8000000 | tf_op jit(solution)/shard_map/pallas_call | solution.py:448
  79.9 3.2 %shard_map.85 = (bf16[256,1536]{1,0:T(8,128)(2,1)}, bf16[256,1536]{1,0:T(8,128)(2,1)}, bf16[256,1536]{1,0:T(8,128)(2,1)}, bf16[256,1536]{1,0:T(8,128)(2,1)}) custom-call(bf16[256,1536]{1,0:T(8,128)(2,1)} %get-tuple-element.8.refs_0_, bf16[256,1536]{1,0:T(8,128)(2,1)} %get-tuple-element.9.refs_1_, bf16[256,1536]{1,0:T(8,128)(2,1)} %get-tuple-element.10.refs_2_, ...), custom_call_target="tpu_custom_call" | custom-call | bytes 6000000 | tf_op jit(solution)/shard_map/pallas_call | solution.py:487

commit v5 on v4

--- a/solution.py
+++ b/solution.py
@@ -137,14 +137,9 @@
                     ).start()
 
     send_kv(0, front, first_recv)
-    send_kv(1, front, first_recv)
     send_kv(0, 1 - front, rest_recv)
     send_qg(0)
-    for h in range(1, HG):
-        if h + 1 < HG:
-            send_kv(h + 1, front, first_recv)
-        send_kv(h, 1 - front, rest_recv)
-        send_qg(h)
+    send_kv(1, front, first_recv)
 
     def span_copy(which, p, h):
         span = group if which == 0 else spans - 1 - group
@@ -211,7 +206,7 @@
                 bias[half, s, :, k * BLK : (k + 1) * BLK] = row
 
     spread(0)
-    spread(1)
+    send_kv(1, 1 - front, rest_recv)
 
     key_at = lax.broadcasted_iota(jnp.int32, (BLK, BLK), 0)
     query_at = lax.broadcasted_iota(jnp.int32, (BLK, BLK), 1)
@@ -338,6 +333,17 @@
     def one_head(h, carry):
         n_low = groups - 1
         gather(h)
+
+        @pl.when(h + 1 < HG)
+        def _():
+            send_qg(h + 1)
+
+            @pl.when(h + 2 < HG)
+            def _():
+                send_kv(h + 2, front, first_recv)
+
+            spread(h + 1)
+
         k_sum = kvs[0:slots, h, 0].reshape(slots * BLK, HS)
         v_sum = kvs[0:slots, h, 1].reshape(slots * BLK, HS)
         k_sum_t = jnp.transpose(k_sum)
@@ -373,7 +379,7 @@
 
         @pl.when(h + 2 < HG)
         def _():
-            spread(h + 2)
+            send_kv(h + 2, 1 - front, rest_recv)
 
         @pl.when(h > 0)
         def _():

time: 83.4 us -> 83.4 us (level)
  no operation moved by 1% of the time
where the time goes in v5:
time: 83.4 us; the launch traced here: 83.1 us
  Pallas kernels  81.1 us (97%)
  local copies, waits for them, and re-layouts  1.37 us (2%)
    pallas_call x1, Pallas kernels, on_device(): pl.pallas_call(functools.partial(kernel, groups, every), out_shape=shapes...  77.9 us
    pallas_call x1, Pallas kernels, on_device(): pl.pallas_call(place, out_shape=shapes, in_specs=[anywhere] * 4, out_spec...  3.18 us

profile of v5, /device:TPU:0, one launch (start us, length us, event | category | flops | bytes accessed | tf_op | source)
XLA Modules:
  0.0 83.1 jit_solution(4350651509580843959)
XLA Ops:
  0.6 1.4 %copy.9.lists = s32[32,4]{1,0:T(8,128)} copy(s32[32,4]{0,1:T(4,128)} %param.9) | data formatting | bytes 1024 | tf_op args[4]
  2.0 77.9 %shard_map.84 = (bf16[256,1536]{1,0:T(8,128)(2,1)}, bf16[256,1536]{1,0:T(8,128)(2,1)}, bf16[256,1536]{1,0:T(8,128)(2,1)}, bf16[256,1536]{1,0:T(8,128)(2,1)}) custom-call(bf16[256,1536]{1,0:T(8,128)(2,1)} %q_in.1, bf16[256,1536]{1,0:T(8,128)(2,1)} %k_in.1, bf16[256,1536]{1,0:T(8,128)(2,1)} %v_in.1, bf16[256,1536]{1,0:T(8,128)(2,1)} %g_in.1, s32[32,4]{1,0:T(8,128)} %copy.9.lists), custom_call_target="tpu_custom_call" | custom-call | flops 6000000000 | bytes 8000000 | tf_op jit(solution)/shard_map/pallas_call | solution.py:454
  79.9 3.2 %shard_map.85 = (bf16[256,1536]{1,0:T(8,128)(2,1)}, bf16[256,1536]{1,0:T(8,128)(2,1)}, bf16[256,1536]{1,0:T(8,128)(2,1)}, bf16[256,1536]{1,0:T(8,128)(2,1)}) custom-call(bf16[256,1536]{1,0:T(8,128)(2,1)} %get-tuple-element.8.refs_0_, bf16[256,1536]{1,0:T(8,128)(2,1)} %get-tuple-element.9.refs_1_, bf16[256,1536]{1,0:T(8,128)(2,1)} %get-tuple-element.10.refs_2_, ...), custom_call_target="tpu_custom_call" | custom-call | bytes 6000000 | tf_op jit(solution)/shard_map/pallas_call | solution.py:493

commit v6 on v5

--- a/solution.py
+++ b/solution.py
@@ -12,7 +12,6 @@
 BLK = 128
 SUMS = 8
 PICKS = 4
-PIECES = 4
 GRP = 4
 HG = H // GRP
 WID = HG * HS
@@ -60,10 +59,10 @@
     every,
     q_in, k_in, v_in, g_in, lists,
     o_out, dq_out, dk_out, dv_out,
-    kv_buf, qg_buf, kvs,
+    kv_all, qg_all, kv_buf, qg_buf, kvs,
     o_buf, dq_buf, dk_buf, dv_buf,
     sacc, gstage, grecv, last_acc, late,
-    bias, in_send, first_recv, rest_recv, qg_recv, loc_kv, loc_qg,
+    bias, load, in_send, first_recv, rest_recv, qg_recv, loc_kv, loc_qg,
     z_send, z_recv, g_send, g_recv, out_send, out_recv, loc_out,
 ):
     spans = 2 * groups
@@ -85,6 +84,16 @@
     def head_cols(m, h):
         return pl.ds(pl.multiple_of((m * HG + h) * HS, HS), HS)
 
+    for i in range(H):
+        cols = pl.ds(i * HS, HS)
+        for half in range(2):
+            rows = pl.ds(half * BLK, BLK)
+            for kv, ref in enumerate((k_in, v_in)):
+                pltpu.make_async_copy(
+                    ref.at[rows, cols], kv_all.at[i, half, kv], load.at[0]
+                ).start()
+        for j, ref in enumerate((q_in, g_in)):
+            pltpu.make_async_copy(ref.at[:, cols], qg_all.at[i, j], load.at[1]).start()
     for h in range(HG):
         cols = head_cols(member, h)
         for half in range(2):
@@ -106,36 +115,35 @@
     front = jnp.where(member < 2, 1, 0)
 
     def send_kv(h, half, recv):
-        rows = pl.ds(pl.multiple_of(half * BLK, BLK), BLK)
         for m in range(GRP):
 
             @pl.when(member != m)
             def _():
-                for kv, ref in enumerate((k_in, v_in)):
-                    pltpu.make_async_remote_copy(
-                        src_ref=ref.at[rows, head_cols(m, h)],
-                        dst_ref=kv_buf.at[member, h, half, kv],
-                        send_sem=in_send.at[kv],
-                        recv_sem=recv.at[h, member],
-                        device_id={"ctx": group * GRP + m},
-                        device_id_type=MESH,
-                    ).start()
+                pltpu.make_async_remote_copy(
+                    src_ref=kv_all.at[m * HG + h, half],
+                    dst_ref=kv_buf.at[member, h, half],
+                    send_sem=in_send.at[0],
+                    recv_sem=recv.at[h, member],
+                    device_id={"ctx": group * GRP + m},
+                    device_id_type=MESH,
+                ).start()
 
     def send_qg(h):
         for m in range(GRP):
 
             @pl.when(member != m)
             def _():
-                for i, ref in enumerate((q_in, g_in)):
-                    pltpu.make_async_remote_copy(
-                        src_ref=ref.at[:, head_cols(m, h)],
-                        dst_ref=qg_buf.at[member, h, i],
-                        send_sem=in_send.at[2 + i],
-                        recv_sem=qg_recv.at[h, member],
-                        device_id={"ctx": group * GRP + m},
-                        device_id_type=MESH,
-                    ).start()
-
+                pltpu.make_async_remote_copy(
+                    src_ref=qg_all.at[m * HG + h],
+                    dst_ref=qg_buf.at[member, h],
+                    send_sem=in_send.at[1],
+                    recv_sem=qg_recv.at[h, member],
+                    device_id={"ctx": group * GRP + m},
+                    device_id_type=MESH,
+                ).start()
+
+    pltpu.make_async_copy(kv_all, kv_all, load.at[0]).wait()
+    pltpu.make_async_copy(qg_all, qg_all, load.at[1]).wait()
     send_kv(0, front, first_recv)
     send_kv(0, 1 - front, rest_recv)
     send_qg(0)
@@ -195,7 +203,7 @@
     for half in range(2):
         for k in range(GRP):
             block = (group if half == 0 else spans - 1 - group) * GRP + k
-            picks = [lists[block, i] for i in range(PICKS)]
+            picks = [lists[i, block] for i in range(PICKS)]
             for s in range(slots):
                 end = s * GRP + GRP - 1
                 seen = end == block - 1
@@ -296,13 +304,13 @@
         )
 
     def send_out(a, src, rows, m, h):
-        cols = pl.ds(pl.multiple_of((member * HG + h) * HS, HS), HS)
+        place_at = member * HG + h
 
         @pl.when(member != m)
         def _():
             pltpu.make_async_remote_copy(
                 src_ref=src,
-                dst_ref=outs[a].at[rows, cols],
+                dst_ref=outs[a].at[place_at, rows, :],
                 send_sem=out_send.at[a],
                 recv_sem=out_recv.at[a],
                 device_id={"ctx": group * GRP + m},
@@ -311,7 +319,7 @@
 
         @pl.when(member == m)
         def _():
-            pltpu.make_async_copy(src, outs[a].at[rows, cols], loc_out.at[a]).start()
+            pltpu.make_async_copy(src, outs[a].at[place_at, rows, :], loc_out.at[a]).start()
 
     def finish_head(h):
         for which in range(2):
@@ -391,9 +399,9 @@
 
     finish_head(HG - 1)
 
-    for a in range(4):
-        away = (k_in, v_in, q_in, g_in)[a].at[:, pl.ds(0, (GRP - 1) * WID)]
-        pltpu.make_async_copy(away, away, in_send.at[a]).wait()
+    for i, ref in enumerate((kv_all, qg_all)):
+        away = ref.at[pl.ds(0, (GRP - 1) * HG)]
+        pltpu.make_async_copy(away, away, in_send.at[i]).wait()
     for p in range(groups):
         for which in range(2):
             for h in range(HG):
@@ -411,8 +419,8 @@
                 grad_copy(s, h).wait_send()
 
     for a in range(4):
-        own = outs[a].at[:, pl.ds(0, WID)]
-        away = outs[a].at[:, pl.ds(0, (GRP - 1) * WID)]
+        own = outs[a].at[pl.ds(0, HG)]
+        away = outs[a].at[pl.ds(0, (GRP - 1) * HG)]
         pltpu.make_async_copy(own, own, loc_out.at[a]).wait()
         pltpu.make_async_copy(away, away, out_send.at[a]).wait()
         pltpu.make_async_copy(away, away, out_recv.at[a]).wait()
@@ -420,25 +428,16 @@
 
 def place(*refs):
     sources, targets, held, arrive, leave = refs[:4], refs[4:8], refs[8], refs[9], refs[10]
-    step = sources[0].shape[0] // PIECES
-    pairs = []
     for a in range(4):
-        for i in range(PIECES):
-            rows = pl.ds(i * step, step)
-            mid = held.at[a, rows]
-            pairs.append(
-                (
-                    pltpu.make_async_copy(sources[a].at[rows], mid, arrive.at[a, i]),
-                    pltpu.make_async_copy(mid, targets[a].at[rows], leave.at[a, i]),
-                )
-            )
-    for load, _ in pairs:
-        load.start()
-    for load, store in pairs:
-        load.wait()
-        store.start()
-    for _, store in pairs:
-        store.wait()
+        for i in range(H):
+            pltpu.make_async_copy(
+                sources[a].at[i], held.at[a, :, pl.ds(i * HS, HS)], arrive.at[a]
+            ).start()
+    for a in range(4):
+        pltpu.make_async_copy(held.at[a], held.at[a], arrive.at[a]).wait()
+        pltpu.make_async_copy(held.at[a], targets[a], leave.at[a]).start()
+    for a in range(4):
+        pltpu.make_async_copy(held.at[a], targets[a], leave.at[a]).wait()
 
 
 def on_device(queries, keys, values, grad_out, summary_lists):
@@ -453,10 +452,12 @@
     shapes = [jax.ShapeDtypeStruct((rows, width), bf16)] * 4
     results = pl.pallas_call(
         functools.partial(kernel, groups, every),
-        out_shape=shapes,
+        out_shape=[jax.ShapeDtypeStruct((H, rows, HS), bf16)] * 4,
         in_specs=[anywhere] * 4 + [pl.BlockSpec(memory_space=pltpu.SMEM)],
         out_specs=[anywhere] * 4,
         scratch_shapes=[
+            pltpu.VMEM((H, 2, 2, BLK, HS), bf16),
+            pltpu.VMEM((H, 2, rows, HS), bf16),
             pltpu.VMEM((GRP, HG, 2, 2, BLK, HS), bf16),
             pltpu.VMEM((GRP, HG, 2, rows, HS), bf16),
             pltpu.VMEM((slots, HG, 2, BLK, HS), bf16),
@@ -469,7 +470,8 @@
             pltpu.VMEM((2, HG, 2, BLK, HS), f32),
             pltpu.VMEM((2, HG, 2, BLK, HS), bf16),
             pltpu.VMEM((2, slots, 1, GRP * BLK), f32),
-            dma((4,)),
+            dma((2,)),
+            dma((2,)),
             dma((HG, GRP)),
             dma((HG, GRP)),
             dma((HG, GRP)),
@@ -489,13 +491,13 @@
         cost_estimate=pl.CostEstimate(
             flops=6 * 10**9, bytes_accessed=8 * 10**6, transcendentals=3 * 10**6
         ),
-    )(queries, keys, values, grad_out, summary_lists)
+    )(queries, keys, values, grad_out, summary_lists.T)
     return pl.pallas_call(
         place,
         out_shape=shapes,
         in_specs=[anywhere] * 4,
         out_specs=[anywhere] * 4,
-        scratch_shapes=[pltpu.VMEM((4, rows, width), bf16), dma((4, PIECES)), dma((4, PIECES))],
+        scratch_shapes=[pltpu.VMEM((4, rows, width), bf16), dma((4,)), dma((4,))],
         compiler_params=pltpu.CompilerParams(vmem_limit_bytes=60 * 1024 * 1024),
         cost_estimate=pl.CostEstimate(flops=0, bytes_accessed=6 * 10**6, transcendentals=0),
     )(*results)

time: 83.4 us -> 81.2 us (0.974)
  local copies, waits for them, and re-layouts: 1.37 us -> 0 us
    unnamed x1 -> x0, local copies, waits for them, and re-layouts: 1.37 us -> none
where the time goes in v6:
time: 81.2 us; the launch traced here: 81 us
  Pallas kernels  80.4 us (99%)
    pallas_call x1, Pallas kernels, on_device(): pl.pallas_call(functools.partial(kernel, groups, every), out_shape=[jax.S...  77.5 us
    pallas_call x1, Pallas kernels, on_device(): pl.pallas_call(place, out_shape=shapes, in_specs=[anywhere] * 4, out_spec...  2.88 us

profile of v6, /device:TPU:0, one launch (start us, length us, event | category | flops | bytes accessed | tf_op | source)
XLA Modules:
  0.0 81.0 jit_solution(6162005240660376441)
XLA Ops:
  0.6 77.5 %shard_map.84 = (bf16[12,256,128]{2,1,0:T(8,128)(2,1)}, bf16[12,256,128]{2,1,0:T(8,128)(2,1)}, bf16[12,256,128]{2,1,0:T(8,128)(2,1)}, bf16[12,256,128]{2,1,0:T(8,128)(2,1)}) custom-call(bf16[256,1536]{1,0:T(8,128)(2,1)} %q_in.1, bf16[256,1536]{1,0:T(8,128)(2,1)} %k_in.1, bf16[256,1536]{1,0:T(8,128)(2,1)} %v_in.1, bf16[256,1536]{1,0:T(8,128)(2,1)} %g_in.1, ...), custom_call_target="tpu_custom_call" | custom-call | flops 6000000000 | bytes 8000000 | tf_op jit(solution)/shard_map/pallas_call | solution.py:453
  78.1 2.9 %shard_map.85 = (bf16[256,1536]{1,0:T(8,128)(2,1)}, bf16[256,1536]{1,0:T(8,128)(2,1)}, bf16[256,1536]{1,0:T(8,128)(2,1)}, bf16[256,1536]{1,0:T(8,128)(2,1)}) custom-call(bf16[12,256,128]{2,1,0:T(8,128)(2,1)} %get-tuple-element.8.refs_0_, bf16[12,256,128]{2,1,0:T(8,128)(2,1)} %get-tuple-element.9.refs_1_, bf16[12,256,128]{2,1,0:T(8,128)(2,1)} %get-tuple-element.10.refs_2_, ...), custom_call_target="tpu_custom_call" | custom-call | bytes 6000000 | tf_op jit(solution)/shard_map/pallas_call | solution.py:495

commit v7 on v6

--- a/solution.py
+++ b/solution.py
@@ -85,15 +85,11 @@
         return pl.ds(pl.multiple_of((m * HG + h) * HS, HS), HS)
 
     for i in range(H):
-        cols = pl.ds(i * HS, HS)
-        for half in range(2):
-            rows = pl.ds(half * BLK, BLK)
-            for kv, ref in enumerate((k_in, v_in)):
-                pltpu.make_async_copy(
-                    ref.at[rows, cols], kv_all.at[i, half, kv], load.at[0]
-                ).start()
+        for j, ref in enumerate((k_in, v_in)):
+            pltpu.make_async_copy(ref.at[:, pl.ds(i * HS, HS)], kv_all.at[i, j], load.at[0]).start()
+    for i in range(H):
         for j, ref in enumerate((q_in, g_in)):
-            pltpu.make_async_copy(ref.at[:, cols], qg_all.at[i, j], load.at[1]).start()
+            pltpu.make_async_copy(ref.at[:, pl.ds(i * HS, HS)], qg_all.at[i, j], load.at[1]).start()
     for h in range(HG):
         cols = head_cols(member, h)
         for half in range(2):
@@ -115,12 +111,13 @@
     front = jnp.where(member < 2, 1, 0)
 
     def send_kv(h, half, recv):
+        rows = pl.ds(pl.multiple_of(half * BLK, BLK), BLK)
         for m in range(GRP):
 
             @pl.when(member != m)
             def _():
                 pltpu.make_async_remote_copy(
-                    src_ref=kv_all.at[m * HG + h, half],
+                    src_ref=kv_all.at[m * HG + h, :, rows, :],
                     dst_ref=kv_buf.at[member, h, half],
                     send_sem=in_send.at[0],
                     recv_sem=recv.at[h, member],
@@ -143,9 +140,9 @@
                 ).start()
 
     pltpu.make_async_copy(kv_all, kv_all, load.at[0]).wait()
-    pltpu.make_async_copy(qg_all, qg_all, load.at[1]).wait()
     send_kv(0, front, first_recv)
     send_kv(0, 1 - front, rest_recv)
+    pltpu.make_async_copy(qg_all, qg_all, load.at[1]).wait()
     send_qg(0)
     send_kv(1, front, first_recv)
 
@@ -456,7 +453,7 @@
         in_specs=[anywhere] * 4 + [pl.BlockSpec(memory_space=pltpu.SMEM)],
         out_specs=[anywhere] * 4,
         scratch_shapes=[
-            pltpu.VMEM((H, 2, 2, BLK, HS), bf16),
+            pltpu.VMEM((H, 2, rows, HS), bf16),
             pltpu.VMEM((H, 2, rows, HS), bf16),
             pltpu.VMEM((GRP, HG, 2, 2, BLK, HS), bf16),
             pltpu.VMEM((GRP, HG, 2, rows, HS), bf16),

time: 81.2 us -> 81.2 us (level)
  no operation moved by 1% of the time
where the time goes in v7:
time: 81.2 us; the launch traced here: 81 us
  Pallas kernels  80.4 us (99%)
    pallas_call x1, Pallas kernels, on_device(): pl.pallas_call(functools.partial(kernel, groups, every), out_shape=[jax.S...  77.5 us
    pallas_call x1, Pallas kernels, on_device(): pl.pallas_call(place, out_shape=shapes, in_specs=[anywhere] * 4, out_spec...  2.88 us

profile of v7, /device:TPU:0, one launch (start us, length us, event | category | flops | bytes accessed | tf_op | source)
XLA Modules:
  0.0 81.0 jit_solution(5875394402345081984)
XLA Ops:
  0.6 77.5 %shard_map.84 = (bf16[12,256,128]{2,1,0:T(8,128)(2,1)}, bf16[12,256,128]{2,1,0:T(8,128)(2,1)}, bf16[12,256,128]{2,1,0:T(8,128)(2,1)}, bf16[12,256,128]{2,1,0:T(8,128)(2,1)}) custom-call(bf16[256,1536]{1,0:T(8,128)(2,1)} %q_in.1, bf16[256,1536]{1,0:T(8,128)(2,1)} %k_in.1, bf16[256,1536]{1,0:T(8,128)(2,1)} %v_in.1, bf16[256,1536]{1,0:T(8,128)(2,1)} %g_in.1, ...), custom_call_target="tpu_custom_call" | custom-call | flops 6000000000 | bytes 8000000 | tf_op jit(solution)/shard_map/pallas_call | solution.py:450
  78.1 2.9 %shard_map.85 = (bf16[256,1536]{1,0:T(8,128)(2,1)}, bf16[256,1536]{1,0:T(8,128)(2,1)}, bf16[256,1536]{1,0:T(8,128)(2,1)}, bf16[256,1536]{1,0:T(8,128)(2,1)}) custom-call(bf16[12,256,128]{2,1,0:T(8,128)(2,1)} %get-tuple-element.8.refs_0_, bf16[12,256,128]{2,1,0:T(8,128)(2,1)} %get-tuple-element.9.refs_1_, bf16[12,256,128]{2,1,0:T(8,128)(2,1)} %get-tuple-element.10.refs_2_, ...), custom_call_target="tpu_custom_call" | custom-call | bytes 6000000 | tf_op jit(solution)/shard_map/pallas_call | solution.py:492
